TPU v7x, 32 devices: a whole 2x2x4 slice. The times are simulated.
32 devices in a mesh: dp: 16 (over z, x, core), fsdp: 2 (over y).
Axes of the slice: x: 2, y: 2, z: 4, core: 2. Of those that a mesh axis runs over, the one named last changes fastest.
Arguments:
- hidden_in: bfloat16 [224, 128, 768], P(('dp', 'fsdp')), may hold values from -100 to 100
- row_counts: int32 [32], P(('dp', 'fsdp')), may hold values from 2 to 7
- buckets: int32 [224], P(('dp', 'fsdp')), may hold values from 0 to 2, as said below
- lengths: int32 [224, 4], P(('dp', 'fsdp')), may hold values from 0 to 128, as said below
- keep_masks: int32 [2, 2, 224, 128, 768], P(None, None, ('dp', 'fsdp')), may hold values 0 or 1
- out_cotangent: bfloat16 [2, 224, 128, 768], P(None, ('dp', 'fsdp')), may hold values from -6 to 6
- w_query: bfloat16 [768, 768], P(('dp', 'fsdp')), may hold values from -0.21875 to 0.21875
- b_query: bfloat16 [768], P(('dp', 'fsdp')), may hold values from -3 to 3
- w_key: bfloat16 [768, 768], P(('dp', 'fsdp')), may hold values from -0.21875 to 0.21875
- w_value: bfloat16 [768, 768], P(('dp', 'fsdp')), may hold values from -0.21875 to 0.21875
- b_value: bfloat16 [768], P(('dp', 'fsdp')), may hold values from -3 to 3
- w_attn_out: bfloat16 [768, 768], P(('dp', 'fsdp')), may hold values from -1.25 to 1.25
- b_attn_out: bfloat16 [768], P(('dp', 'fsdp')), may hold values from -3 to 3
- norm1_gain: bfloat16 [768], P(('dp', 'fsdp')), may hold values from 0.099609375 to 1.8984375
- norm1_bias: bfloat16 [768], P(('dp', 'fsdp')), may hold values from -2 to 2
- w_inner: bfloat16 [768, 3072], P(('dp', 'fsdp')), may hold values from -0.21875 to 0.21875
- b_inner: bfloat16 [3072], P(('dp', 'fsdp')), may hold values from -3 to 3
- w_outer: bfloat16 [3072, 768], P(('dp', 'fsdp')), may hold values from -0.109375 to 0.109375
- b_outer: bfloat16 [768], P(('dp', 'fsdp')), may hold values from -3 to 3
- norm2_gain: bfloat16 [768], P(('dp', 'fsdp')), may hold values from 0.099609375 to 1.8984375
- norm2_bias: bfloat16 [768], P(('dp', 'fsdp')), may hold values from -2 to 2
- w_pool: bfloat16 [768, 768], P(('dp', 'fsdp')), may hold values from -0.21875 to 0.21875
- b_pool: bfloat16 [768], P(('dp', 'fsdp')), may hold values from -2 to 2
- log_temp: float32 [1], replicated, may hold values from -1.9 to -1.4
Outputs:
- loss: float32 [1], replicated
- outputs: bfloat16 [2, 224, 128, 768], P(None, ('dp', 'fsdp'))
- input_grad: float32 [224, 128, 768], P(('dp', 'fsdp'))
- grad_w_query: float32 [768, 768], P(('dp', 'fsdp'))
- grad_b_query: float32 [768], P(('dp', 'fsdp'))
- grad_w_key: float32 [768, 768], P(('dp', 'fsdp'))
- grad_w_value: float32 [768, 768], P(('dp', 'fsdp'))
- grad_b_value: float32 [768], P(('dp', 'fsdp'))
- grad_w_attn_out: float32 [768, 768], P(('dp', 'fsdp'))
- grad_b_attn_out: float32 [768], P(('dp', 'fsdp'))
- grad_norm1_gain: float32 [768], P(('dp', 'fsdp'))
- grad_norm1_bias: float32 [768], P(('dp', 'fsdp'))
- grad_w_inner: float32 [768, 3072], P(('dp', 'fsdp'))
- grad_b_inner: float32 [3072], P(('dp', 'fsdp'))
- grad_w_outer: float32 [3072, 768], P(('dp', 'fsdp'))
- grad_b_outer: float32 [768], P(('dp', 'fsdp'))
- grad_norm2_gain: float32 [768], P(('dp', 'fsdp'))
- grad_norm2_bias: float32 [768], P(('dp', 'fsdp'))
- grad_w_pool: float32 [768, 768], P(('dp', 'fsdp'))
- grad_b_pool: float32 [768], P(('dp', 'fsdp'))
- log_temp_grad: float32 [1], replicated
Inputs may be any that keep to these rules, and one draw needn't show every extreme that they name: `buckets`: a row of bucket b holds 4 >> b sentences of 128 >> (3 - b) + 1 to 128 >> (2 - b) tokens. Entry k of a row is its k-th sentence's length for k < 4 >> b and 0 after; a row's lengths sum to at most 128.
All inputs are finite; a program needn't handle non-finite values. No bound on the sum of `keep_masks` on one device may be relied on, other than what follows from the above.
Results may differ from a plain program's by a relative error of at most 0.014.
Values may be sent and summed in bfloat16 or wider, within the bound.
No kernel may reach another device: no remote copies, remote signals or barrier semaphores. Data moves between devices by JAX's collectives and lax.ppermute only.
A program may use at most 320 MiB of HBM per device.

v0:
```python
import jax
import jax.numpy as jnp
from jax import lax
from jax.sharding import PartitionSpec as P

HEADS = 12


precise = lax.Precision.HIGHEST
keep_scale = 1.0 / 0.9
inv_root_two = 0.7071067811865476
inv_root_tau = 0.3989422804014327


def matmul(left, right):
    return jnp.dot(left, right, preferred_element_type=jnp.float32)


def against(left, right):
    return lax.dot_general(
        left, right, (((1,), (1,)), ((), ())), preferred_element_type=jnp.float32
    )


def across(left, right):
    return lax.dot_general(
        left, right, (((0,), (0,)), ((), ())), preferred_element_type=jnp.float32
    )


def layout(row_counts, buckets, lengths, row_len):
    slot_count = buckets.shape[0]
    live_rows = jnp.arange(slot_count, dtype=jnp.int32) < row_counts[0]
    sent_count = jnp.right_shift(jnp.int32(4), buckets)
    slot_ids = jnp.arange(4, dtype=jnp.int32)
    held_slots = (slot_ids[None, :] < sent_count[:, None]) & live_rows[:, None]
    sizes_used = jnp.where(held_slots, lengths, 0)
    finish = jnp.cumsum(sizes_used, axis=1, dtype=jnp.int32)
    starts = finish - sizes_used
    places = jnp.arange(row_len, dtype=jnp.int32)
    segment = jnp.sum((places[None, :, None] >= finish[:, None, :]).astype(jnp.int32), axis=2)
    cls_table = ((places[None, None, :] == starts[:, :, None]) & held_slots[:, :, None]).astype(
        jnp.float32
    )
    return (segment, (segment < 4).astype(jnp.float32), cls_table, held_slots.astype(jnp.float32))


def norm_fwd(hidden, gain, shift):
    centre = jnp.mean(hidden, axis=-1, keepdims=True)
    offset = hidden - centre
    spread = jnp.mean(offset * offset, axis=-1, keepdims=True)
    rscale = lax.rsqrt(spread + 1e-06)
    normed = offset * rscale
    return (normed * gain + shift, normed, rscale)


def norm_back(grad_out, normed, rscale, gain):
    grad_norm = grad_out * gain
    mean_grad = jnp.mean(grad_norm, axis=-1, keepdims=True)
    mean_cross = jnp.mean(grad_norm * normed, axis=-1, keepdims=True)
    grad_in = rscale * (grad_norm - mean_grad - normed * mean_cross)
    return (grad_in, jnp.sum(grad_out * normed, axis=(0, 1)), jnp.sum(grad_out, axis=(0, 1)))


def anchor_side(anchors, partners, partners_all, flags, column_ok, inv_temp):
    held_total = jnp.sum(column_ok)
    logits = against(anchors, partners_all) * inv_temp
    logits = jnp.where(column_ok[None, :] > 0, logits, -1e30)
    sim_peak = jnp.max(logits, axis=-1, keepdims=True)
    sim_total = sim_peak + jnp.log(jnp.sum(jnp.exp(logits - sim_peak), axis=-1, keepdims=True))
    anchors_f = anchors.astype(jnp.float32)
    partners_f = partners.astype(jnp.float32)
    positive = jnp.sum(anchors_f * partners_f, axis=-1) * inv_temp
    row_weight = flags / held_total
    loss_part = jnp.sum(row_weight * (sim_total[:, 0] - positive))
    shares = jnp.exp(logits - sim_total) * row_weight[:, None]
    temp_part = jnp.sum(row_weight * positive) - jnp.sum(
        shares * jnp.where(column_ok[None, :] > 0, logits, 0.0)
    )
    grad_anchor = inv_temp * (
        jnp.dot(shares, partners_all.astype(jnp.float32), precision=precise)
        - row_weight[:, None] * partners_f
    )
    return (loss_part, temp_part, grad_anchor, sim_total[:, 0], row_weight, held_total, anchors_f)


def partner_side(partners, anchors_all, totals_all, anchor_ok, flags, held_total, inv_temp):
    back_logits = against(partners, anchors_all) * inv_temp
    back_shares = (
        jnp.exp(back_logits - totals_all[None, :])
        * (anchor_ok / held_total)[None, :]
        * flags[:, None]
    )
    return inv_temp * jnp.dot(back_shares, anchors_all.astype(jnp.float32), precision=precise)


def body(
    hidden_in,
    row_counts,
    buckets,
    lengths,
    keep_masks,
    out_cotangent,
    w_query,
    b_query,
    w_key,
    w_value,
    b_value,
    w_attn_out,
    b_attn_out,
    norm1_gain,
    norm1_bias,
    w_inner,
    b_inner,
    w_outer,
    b_outer,
    norm2_gain,
    norm2_bias,
    w_pool,
    b_pool,
    log_temp,
):
    gathered = (
        lax.all_gather(w_query, ("dp", "fsdp"), axis=0, tiled=True),
        lax.all_gather(b_query, ("dp", "fsdp"), axis=0, tiled=True),
        lax.all_gather(w_key, ("dp", "fsdp"), axis=0, tiled=True),
        lax.all_gather(w_value, ("dp", "fsdp"), axis=0, tiled=True),
        lax.all_gather(b_value, ("dp", "fsdp"), axis=0, tiled=True),
        lax.all_gather(w_attn_out, ("dp", "fsdp"), axis=0, tiled=True),
        lax.all_gather(b_attn_out, ("dp", "fsdp"), axis=0, tiled=True),
        lax.all_gather(norm1_gain, ("dp", "fsdp"), axis=0, tiled=True),
        lax.all_gather(norm1_bias, ("dp", "fsdp"), axis=0, tiled=True),
        lax.all_gather(w_inner, ("dp", "fsdp"), axis=0, tiled=True),
        lax.all_gather(b_inner, ("dp", "fsdp"), axis=0, tiled=True),
        lax.all_gather(w_outer, ("dp", "fsdp"), axis=0, tiled=True),
        lax.all_gather(b_outer, ("dp", "fsdp"), axis=0, tiled=True),
        lax.all_gather(norm2_gain, ("dp", "fsdp"), axis=0, tiled=True),
        lax.all_gather(norm2_bias, ("dp", "fsdp"), axis=0, tiled=True),
        lax.all_gather(w_pool, ("dp", "fsdp"), axis=0, tiled=True),
        lax.all_gather(b_pool, ("dp", "fsdp"), axis=0, tiled=True),
    )
    (
        query_weight,
        query_bias,
        key_weight,
        value_weight,
        value_bias,
        out_weight,
        out_bias,
        gain_one,
        shift_one,
        inner_weight,
        inner_bias,
        outer_weight,
        outer_bias,
        gain_two,
        shift_two,
        pool_weight,
        pool_bias,
    ) = gathered
    slots, row_len, width = hidden_in.shape
    head_dim = width // HEADS
    tokens = slots * row_len
    segment, token_ok, cls_table, held_slots = layout(row_counts, buckets, lengths, row_len)
    flat_in = hidden_in.reshape(tokens, width)

    def heads_of(matrix):
        return matrix.reshape(slots, row_len, HEADS, head_dim)

    same_seg = (segment[:, :, None] == segment[:, None, :])[:, None]

    def scores_of(query_heads, key_heads):
        raw_scores = (
            jnp.einsum(
                "slhd,smhd->shlm", query_heads, key_heads, preferred_element_type=jnp.float32
            )
            * 0.125
        )
        return jnp.where(same_seg, raw_scores, -1e30)

    query_low = (matmul(flat_in, query_weight) + query_bias).astype(jnp.bfloat16)
    keys_low = matmul(flat_in, key_weight).astype(jnp.bfloat16)
    values_low = (matmul(flat_in, value_weight) + value_bias).astype(jnp.bfloat16)
    scores = scores_of(heads_of(query_low), heads_of(keys_low))
    peak = jnp.max(scores, axis=-1, keepdims=True)
    log_total = peak + jnp.log(jnp.sum(jnp.exp(scores - peak), axis=-1, keepdims=True))
    probs_low = jnp.exp(scores - log_total).astype(jnp.bfloat16)
    attended = (
        jnp.einsum(
            "shlm,smhd->slhd", probs_low, heads_of(values_low), preferred_element_type=jnp.float32
        )
        .reshape(tokens, width)
        .astype(jnp.bfloat16)
    )
    branch = matmul(attended, out_weight) + out_bias
    keeps = keep_masks.reshape(2, 2, tokens, width).astype(jnp.float32) * keep_scale
    residual = flat_in.astype(jnp.float32)
    first_sum = residual[None] + branch[None] * keeps[:, 0]
    normed_one, unit_one, scale_one = norm_fwd(first_sum, gain_one, shift_one)
    inner_in = normed_one.astype(jnp.bfloat16).reshape(2 * tokens, width)
    inner = matmul(inner_in, inner_weight) + inner_bias
    active = jax.nn.gelu(inner, approximate=False).astype(jnp.bfloat16)
    outer = (matmul(active, outer_weight) + outer_bias).reshape(2, tokens, width)
    second_sum = normed_one + outer * keeps[:, 1]
    normed_two, unit_two, scale_two = norm_fwd(second_sum, gain_two, shift_two)
    result = normed_two.astype(jnp.bfloat16).reshape(2, slots, row_len, width)
    sent_slots = slots * 4
    cls_rows = (
        jnp.einsum(
            "skl,vsld->vskd",
            cls_table.astype(jnp.bfloat16),
            result,
            preferred_element_type=jnp.float32,
        )
        .astype(jnp.bfloat16)
        .reshape(2 * sent_slots, width)
    )
    pre_pool = matmul(cls_rows, pool_weight) + pool_bias
    pooled = jnp.tanh(pre_pool)
    pool_scale = lax.rsqrt(jnp.sum(pooled * pooled, axis=-1, keepdims=True) + 1e-06)
    unit_low = (pooled * pool_scale).astype(jnp.bfloat16)
    anchors = unit_low[:sent_slots]
    partners = unit_low[sent_slots:]
    flags = held_slots.reshape(sent_slots)
    inv_temp = jnp.exp(-log_temp[0])
    again = (
        lax.all_gather(w_query, ("dp", "fsdp"), axis=0, tiled=True),
        lax.all_gather(b_query, ("dp", "fsdp"), axis=0, tiled=True),
        lax.all_gather(w_key, ("dp", "fsdp"), axis=0, tiled=True),
        lax.all_gather(w_value, ("dp", "fsdp"), axis=0, tiled=True),
        lax.all_gather(b_value, ("dp", "fsdp"), axis=0, tiled=True),
        lax.all_gather(w_attn_out, ("dp", "fsdp"), axis=0, tiled=True),
        lax.all_gather(b_attn_out, ("dp", "fsdp"), axis=0, tiled=True),
        lax.all_gather(norm1_gain, ("dp", "fsdp"), axis=0, tiled=True),
        lax.all_gather(norm1_bias, ("dp", "fsdp"), axis=0, tiled=True),
        lax.all_gather(w_inner, ("dp", "fsdp"), axis=0, tiled=True),
        lax.all_gather(b_inner, ("dp", "fsdp"), axis=0, tiled=True),
        lax.all_gather(w_outer, ("dp", "fsdp"), axis=0, tiled=True),
        lax.all_gather(b_outer, ("dp", "fsdp"), axis=0, tiled=True),
        lax.all_gather(norm2_gain, ("dp", "fsdp"), axis=0, tiled=True),
        lax.all_gather(norm2_bias, ("dp", "fsdp"), axis=0, tiled=True),
        lax.all_gather(w_pool, ("dp", "fsdp"), axis=0, tiled=True),
        lax.all_gather(b_pool, ("dp", "fsdp"), axis=0, tiled=True),
    )
    (
        query_weight,
        query_bias,
        key_weight,
        value_weight,
        value_bias,
        out_weight,
        out_bias,
        gain_one,
        shift_one,
        inner_weight,
        inner_bias,
        outer_weight,
        outer_bias,
        gain_two,
        shift_two,
        pool_weight,
        pool_bias,
    ) = again
    anchors_all, partners_all, flags_all = (
        lax.all_gather(anchors, ("dp", "fsdp"), axis=0, tiled=True),
        lax.all_gather(partners, ("dp", "fsdp"), axis=0, tiled=True),
        lax.all_gather(flags.astype(jnp.bfloat16), ("dp", "fsdp"), axis=0, tiled=True),
    )
    column_ok = flags_all.astype(jnp.float32)
    loss_part, temp_part, grad_anchor, sim_total, row_weight, held_total, anchors_f = anchor_side(
        anchors, partners, partners_all, flags, column_ok, inv_temp
    )
    totals_all = lax.all_gather(sim_total, ("dp", "fsdp"), axis=0, tiled=True)
    grad_partner = partner_side(
        partners, anchors_all, totals_all, column_ok, flags, held_total, inv_temp
    )
    grad_partner = grad_partner - inv_temp * row_weight[:, None] * anchors_f
    totals = lax.psum((loss_part, temp_part), ("dp", "fsdp"))
    grad_unit = jnp.concatenate([grad_anchor, grad_partner], axis=0)
    grad_pooled = pool_scale * grad_unit - pooled * (
        pool_scale * pool_scale * pool_scale
    ) * jnp.sum(pooled * grad_unit, axis=-1, keepdims=True)
    grad_pre = (grad_pooled * (1.0 - pooled * pooled)).astype(jnp.bfloat16)
    grad_pool_bias = jnp.sum(grad_pre.astype(jnp.float32), axis=0)
    grad_pool_weight = across(cls_rows, grad_pre)
    grad_cls = against(grad_pre, pool_weight).reshape(2, slots, 4, width)
    grad_result = out_cotangent.astype(jnp.float32).reshape(2, tokens, width) * token_ok.reshape(
        1, tokens, 1
    ) + jnp.einsum("skl,vskd->vsld", cls_table, grad_cls, precision=precise).reshape(
        2, tokens, width
    )
    grad_second, grad_gain_two, grad_shift_two = norm_back(
        grad_result, unit_two, scale_two, gain_two
    )
    grad_outer = (grad_second * keeps[:, 1]).astype(jnp.bfloat16).reshape(2 * tokens, width)
    grad_outer_bias = jnp.sum(grad_outer.astype(jnp.float32), axis=0)
    grad_outer_weight = across(active, grad_outer)
    grad_active = against(grad_outer, outer_weight)
    slope = (
        0.5 * (1.0 + lax.erf(inner * inv_root_two))
        + inner * jnp.exp(-0.5 * inner * inner) * inv_root_tau
    )
    grad_inner = (grad_active * slope).astype(jnp.bfloat16)
    grad_inner_bias = jnp.sum(grad_inner.astype(jnp.float32), axis=0)
    grad_inner_weight = across(inner_in, grad_inner)
    grad_normed = against(grad_inner, inner_weight).reshape(2, tokens, width) + grad_second
    grad_first, grad_gain_one, grad_shift_one = norm_back(
        grad_normed, unit_one, scale_one, gain_one
    )
    grad_branch = jnp.sum(grad_first * keeps[:, 0], axis=0).astype(jnp.bfloat16)
    grad_out_bias = jnp.sum(grad_branch.astype(jnp.float32), axis=0)
    grad_out_weight = across(attended, grad_branch)
    grad_attended = against(grad_branch, out_weight).astype(jnp.bfloat16)
    scores_again = scores_of(heads_of(query_low), heads_of(keys_low))
    probs_again = jnp.exp(scores_again - log_total)
    probs_round = probs_again.astype(jnp.bfloat16)
    grad_probs = jnp.einsum(
        "slhd,smhd->shlm",
        heads_of(grad_attended),
        heads_of(values_low),
        preferred_element_type=jnp.float32,
    )
    grad_values = (
        jnp.einsum(
            "shlm,slhd->smhd",
            probs_round,
            heads_of(grad_attended),
            preferred_element_type=jnp.float32,
        )
        .reshape(tokens, width)
        .astype(jnp.bfloat16)
    )
    grad_scores = (
        probs_again * (grad_probs - jnp.sum(grad_probs * probs_again, axis=-1, keepdims=True))
    ).astype(jnp.bfloat16)
    grad_query = (
        (
            jnp.einsum(
                "shlm,smhd->slhd",
                grad_scores,
                heads_of(keys_low),
                preferred_element_type=jnp.float32,
            )
            * 0.125
        )
        .reshape(tokens, width)
        .astype(jnp.bfloat16)
    )
    grad_keys = (
        (
            jnp.einsum(
                "shlm,slhd->smhd",
                grad_scores,
                heads_of(query_low),
                preferred_element_type=jnp.float32,
            )
            * 0.125
        )
        .reshape(tokens, width)
        .astype(jnp.bfloat16)
    )
    grad_query_weight = across(flat_in, grad_query)
    grad_query_bias = jnp.sum(grad_query.astype(jnp.float32), axis=0)
    grad_key_weight = across(flat_in, grad_keys)
    grad_value_weight = across(flat_in, grad_values)
    grad_value_bias = jnp.sum(grad_values.astype(jnp.float32), axis=0)
    input_grad = (
        jnp.sum(grad_first, axis=0)
        + against(grad_query, query_weight)
        + against(grad_keys, key_weight)
        + against(grad_values, value_weight)
    )
    input_grad = input_grad.reshape(slots, row_len, width)
    shards_out = (
        lax.psum_scatter(grad_query_weight, ("dp", "fsdp"), scatter_dimension=0, tiled=True),
        lax.psum_scatter(grad_query_bias, ("dp", "fsdp"), scatter_dimension=0, tiled=True),
        lax.psum_scatter(grad_key_weight, ("dp", "fsdp"), scatter_dimension=0, tiled=True),
        lax.psum_scatter(grad_value_weight, ("dp", "fsdp"), scatter_dimension=0, tiled=True),
        lax.psum_scatter(grad_value_bias, ("dp", "fsdp"), scatter_dimension=0, tiled=True),
        lax.psum_scatter(grad_out_weight, ("dp", "fsdp"), scatter_dimension=0, tiled=True),
        lax.psum_scatter(grad_out_bias, ("dp", "fsdp"), scatter_dimension=0, tiled=True),
        lax.psum_scatter(grad_gain_one, ("dp", "fsdp"), scatter_dimension=0, tiled=True),
        lax.psum_scatter(grad_shift_one, ("dp", "fsdp"), scatter_dimension=0, tiled=True),
        lax.psum_scatter(grad_inner_weight, ("dp", "fsdp"), scatter_dimension=0, tiled=True),
        lax.psum_scatter(grad_inner_bias, ("dp", "fsdp"), scatter_dimension=0, tiled=True),
        lax.psum_scatter(grad_outer_weight, ("dp", "fsdp"), scatter_dimension=0, tiled=True),
        lax.psum_scatter(grad_outer_bias, ("dp", "fsdp"), scatter_dimension=0, tiled=True),
        lax.psum_scatter(grad_gain_two, ("dp", "fsdp"), scatter_dimension=0, tiled=True),
        lax.psum_scatter(grad_shift_two, ("dp", "fsdp"), scatter_dimension=0, tiled=True),
        lax.psum_scatter(grad_pool_weight, ("dp", "fsdp"), scatter_dimension=0, tiled=True),
        lax.psum_scatter(grad_pool_bias, ("dp", "fsdp"), scatter_dimension=0, tiled=True),
    )
    return (
        totals[0].reshape(1),
        result,
        input_grad,
        shards_out[0],
        shards_out[1],
        shards_out[2],
        shards_out[3],
        shards_out[4],
        shards_out[5],
        shards_out[6],
        shards_out[7],
        shards_out[8],
        shards_out[9],
        shards_out[10],
        shards_out[11],
        shards_out[12],
        shards_out[13],
        shards_out[14],
        shards_out[15],
        shards_out[16],
        totals[1].reshape(1),
    )


def solution(mesh):
    in_specs = (
        P(("dp", "fsdp"), None, None),
        P(("dp", "fsdp")),
        P(("dp", "fsdp")),
        P(("dp", "fsdp"), None),
        P(None, None, ("dp", "fsdp"), None, None),
        P(None, ("dp", "fsdp"), None, None),
        P(("dp", "fsdp"), None),
        P(("dp", "fsdp")),
        P(("dp", "fsdp"), None),
        P(("dp", "fsdp"), None),
        P(("dp", "fsdp")),
        P(("dp", "fsdp"), None),
        P(("dp", "fsdp")),
        P(("dp", "fsdp")),
        P(("dp", "fsdp")),
        P(("dp", "fsdp"), None),
        P(("dp", "fsdp")),
        P(("dp", "fsdp"), None),
        P(("dp", "fsdp")),
        P(("dp", "fsdp")),
        P(("dp", "fsdp")),
        P(("dp", "fsdp"), None),
        P(("dp", "fsdp")),
        P(),
    )
    out_specs = (
        P(),
        P(None, ("dp", "fsdp"), None, None),
        P(("dp", "fsdp"), None, None),
        P(("dp", "fsdp"), None),
        P(("dp", "fsdp")),
        P(("dp", "fsdp"), None),
        P(("dp", "fsdp"), None),
        P(("dp", "fsdp")),
        P(("dp", "fsdp"), None),
        P(("dp", "fsdp")),
        P(("dp", "fsdp")),
        P(("dp", "fsdp")),
        P(("dp", "fsdp"), None),
        P(("dp", "fsdp")),
        P(("dp", "fsdp"), None),
        P(("dp", "fsdp")),
        P(("dp", "fsdp")),
        P(("dp", "fsdp")),
        P(("dp", "fsdp"), None),
        P(("dp", "fsdp")),
        P(),
    )
    return jax.shard_map(body, mesh=mesh, in_specs=in_specs, out_specs=out_specs, check_vma=False)
```

profile of v0, /device:TPU:0, one launch (start us, length us, event | category | flops | bytes accessed | tf_op | source)
XLA Modules:
  0.0 1365.6 jit_solution(6976542198261489701)
XLA Ops:
  23.6 42.4 %all-reduce.23 = (bf16[896]{0:T(1024)(128)(2,1)}, bf16[768]{0:T(1024)(128)(2,1)S(1)}, bf16[768]{0:T(1024)(128)(2,1)S(1)}, bf16[768]{0:T(1024)(128)(2,1)S(1)}, bf...) all-reduce(bf16[896]{0:T(1024)(128)(2,1)S(1)} %dynamic-update-slice, ...), channel_id=1, replica_groups=mesh['dp'=16,'fsdp'=2] {'dp','fsdp'}, use_global_device_ids=true, to_apply=%add | all-reduce | flops 10880 | bytes 43520
  71.3 9.7 convert_multiply_fusion
  107.7 16.2 %all-gather.16.cloned.1.call-done = bf16[768,768]{1,0:T(8,128)(2,1)} async-done(((bf16[24,768]{1,0:T(8,128)(2,1)}), bf16[768,768]{1,0:T(8,128)(2,1)}) %all-gather.16.cloned.1.call-update) | async-done | bytes 1179664 | tf_op jit(solution)/shard_map/all_gather | solution.py:126
  138.6 41.3 %all-gather.12.cloned.1.call-done = bf16[768,768]{1,0:T(8,128)(2,1)} async-done(((bf16[24,768]{1,0:T(8,128)(2,1)}), bf16[768,768]{1,0:T(8,128)(2,1)}) %all-gather.12.cloned.1.call-update) | async-done | bytes 1179664 | tf_op jit(solution)/shard_map/all_gather | solution.py:127
  191.7 44.1 %all-gather.18.cloned.1.call-done = bf16[768,768]{1,0:T(8,128)(2,1)} async-done(((bf16[24,768]{1,0:T(8,128)(2,1)}), bf16[768,768]{1,0:T(8,128)(2,1)}) %all-gather.18.cloned.1.call-update) | async-done | bytes 1179664 | tf_op jit(solution)/shard_map/all_gather | solution.py:129
  253.2 47.9 %all-gather.20.cloned.1.call-done = bf16[768,3072]{1,0:T(8,128)(2,1)} async-done(((bf16[24,3072]{1,0:T(8,128)(2,1)}), bf16[768,3072]{1,0:T(8,128)(2,1)}) %all-gather.20.cloned.1.call-update) | async-done | bytes 4718608 | tf_op jit(solution)/shard_map/all_gather | solution.py:133
  301.2 58.3 %fusion.2 = (bf16[1792,3072]{1,0:T(8,128)(2,1)}, f32[1792,3072]{1,0:T(8,128)}) fusion(f32[3072]{0:T(1024)S(1)} %convert_element_type.237, bf16[768,3072]{1,0:T(8,128)(2,1)} %all-gather.20.cloned.1.call-done, f32[1792,768]{1,0:T(8,128)} %fusion.37, f32[768]{0:T(1024)S(1)} %convert_element_type.235, f32[768]{0:T(1024)S(1)} %convert_element_type.234), kind=kOutput, calls=%fused_computation.4 | convolution fusion | flops 8823177216 | bytes 43272192 | tf_op jit(solution)/shard_map/dot_general | solution.py:16
  366.5 14.7 %convolution_add_fusion = f32[1792,768]{1,0:T(8,128)} fusion(bf16[1792,3072]{1,0:T(8,128)(2,1)} %get-tuple-element.176, bf16[3072,768]{1,0:T(8,128)(2,1)} %all-gather.22.cloned.1.call-done, f32[768]{0:T(1024)S(1)} %copy-done.65), kind=kOutput, calls=%fused_computation.93 | convolution fusion | flops 8457093120 | bytes 21236736 | tf_op jit(solution)/shard_map/dot_general | solution.py:16
  403.9 18.5 %all-gather.24.cloned.1.call-done = bf16[768,768]{1,0:T(8,128)(2,1)} async-done(((bf16[24,768]{1,0:T(8,128)(2,1)}), bf16[768,768]{1,0:T(8,128)(2,1)}) %all-gather.24.cloned.1.call-update) | async-done | bytes 1179664 | tf_op jit(solution)/shard_map/all_gather | solution.py:139
  433.9 46.0 %all-gather.26.cloned.1.call-done = bf16[32,28,768]{2,1,0:T(8,128)(2,1)} async-done(((bf16[1,28,768]{2,1,0:T(8,128)(2,1)}), bf16[32,28,768]{2,1,0:T(8,128)(2,1)}) %all-gather.26.cloned.1.call-update) | async-done | bytes 1376272 | tf_op jit(solution)/shard_map/all_gather | solution.py:266
  485.5 38.9 %all-reduce.11 = f32[896]{0:T(1024)S(1)} all-reduce(f32[896]{0:T(1024)S(1)} %get-tuple-element.145), channel_id=1, replica_groups=mesh['dp'=16,'fsdp'=2] {'dp','fsdp'}, use_global_device_ids=true, to_apply=%add.11 | all-reduce | flops 896 | bytes 7168
  527.1 10.4 all-gather.28.cloned.1.call-done
  560.8 13.5 convert_reduce_fusion.1
  574.3 21.4 %convert_reduce_fusion = (f32[3072]{0:T(1024)S(1)}, bf16[1792,3072]{1,0:T(8,128)(2,1)}) fusion(f32[1792,3072]{1,0:T(8,128)} %get-tuple-element.177, f32[3072]{0:T(1024)S(1)} %convert_element_type.237, bf16[1792,768]{1,0:T(8,128)(2,1)S(1)} %get-tuple-element.143, bf16[3072,768]{1,0:T(8,128)(2,1)} %all-gather.22.cloned.1.call-done), kind=kOutput, calls=%fused_computation.11 | convolution fusion | flops 8527279104 | bytes 40525824 | tf_op jit(solution)/shard_map/dot_general | solution.py:20
  595.7 16.4 %fusion.137 = (f32[1792,768]{1,0:T(8,128)}, f32[1792,768]{1,0:T(8,128)}) fusion(f32[1792,768]{1,0:T(8,128)} %get-tuple-element.144, bf16[1792,3072]{1,0:T(8,128)(2,1)} %get-tuple-element.192, bf16[768,3072]{1,0:T(8,128)(2,1)} %all-gather.20.cloned.1.call-done), kind=kOutput, calls=%fused_computation.235 | convolution fusion | flops 8457093120 | bytes 32243712 | tf_op jit(solution)/shard_map/dot_general | solution.py:20
  615.9 13.3 fusion.127
  687.6 13.9 %fusion.139 = f32[3072,768]{1,0:T(8,128)} fusion(bf16[1792,3072]{1,0:T(8,128)(2,1)} %get-tuple-element.176, bf16[1792,768]{1,0:T(8,128)(2,1)S(1)} %copy-done.29), kind=kOutput, calls=%fused_computation.237 | convolution fusion | flops 8455716864 | bytes 23199744 | tf_op jit(solution)/shard_map/dot_general | solution.py:26
  701.6 15.5 %fusion.95 = f32[768,3072]{1,0:T(8,128)} fusion(bf16[1792,3072]{1,0:T(8,128)(2,1)} %get-tuple-element.192, f32[1792,768]{1,0:T(8,128)} %fusion.37, f32[768]{0:T(1024)S(1)} %convert_element_type.235, f32[768]{0:T(1024)S(1)} %convert_element_type.234), kind=kOutput, calls=%fused_computation.161 | convolution fusion | flops 8459845632 | bytes 25958400 | tf_op jit(solution)/shard_map/dot_general | solution.py:26
  724.4 40.7 %all-reduce.22 = (f32[1]{0:T(128)}, f32[768]{0:T(1024)S(1)}, f32[768]{0:T(1024)S(1)}, f32[768]{0:T(1024)S(1)}, f32[768]{0:T(1024)S(1)}, /*index=5*/f32[768]{0:T(...) all-reduce(f32[1]{0:T(128)} %bitcast.23, ...), channel_id=1, replica_groups=mesh['dp'=16,'fsdp'=2] {'dp','fsdp'}, use_global_device_ids=true, to_apply=%region_14.15 | all-reduce | flops 9986 | bytes 79888 | tf_op jit(solution)/shard_map/psum | solution.py:278
  779.5 88.0 %reduce-scatter.24.cloned.1.call-done = f32[24,768]{1,0:T(8,128)} async-done(((f32[768,768]{1,0:T(8,128)}), f32[24,768]{1,0:T(8,128)}) %reduce-scatter.24.cloned.1.call-update) | async-done | bytes 73744
  867.5 104.8 %reduce-scatter.26.cloned.1.call-done = f32[24,768]{1,0:T(8,128)} async-done(((f32[768,768]{1,0:T(8,128)}), f32[24,768]{1,0:T(8,128)}) %reduce-scatter.26.cloned.1.call-update) | async-done | bytes 73744
  972.3 103.8 %reduce-scatter.22.cloned.1.call-done = f32[24,768]{1,0:T(8,128)} async-done(((f32[768,768]{1,0:T(8,128)}), f32[24,768]{1,0:T(8,128)}) %reduce-scatter.22.cloned.1.call-update) | async-done | bytes 73744
  1076.1 141.8 %reduce-scatter.18.cloned.1.call-done = f32[96,768]{1,0:T(8,128)} async-done(((f32[3072,768]{1,0:T(8,128)}), f32[96,768]{1,0:T(8,128)}) %reduce-scatter.18.cloned.1.call-update) | async-done | bytes 294928 | tf_op jit(solution)/shard_map/reduce_scatter | solution.py:386
  1217.9 140.9 %reduce-scatter.16.cloned.1.call-done = f32[24,3072]{1,0:T(8,128)} async-done(((f32[768,3072]{1,0:T(8,128)}), f32[24,3072]{1,0:T(8,128)}) %reduce-scatter.16.cloned.1.call-update) | async-done | bytes 294928 | tf_op jit(solution)/shard_map/reduce_scatter | solution.py:384
  (356 shorter events, 244.3 us)
Async XLA Ops:
  7.2 62.4 %copy-start.23 = (bf16[7,128,768]{2,1,0:T(8,128)(2,1)S(1)}, bf16[7,128,768]{2,1,0:T(8,128)(2,1)}, u32[]{:S(2)}) copy-start(bf16[7,128,768]{2,1,0:T(8,128)(2,1)} %param.24) | copy-start | bytes 4128772
  7.2 91.1 %all-gather.14.cloned.1.call-start = ((), (), s32[]{:S(2)}) async-start(), calls=%async_computation.8 | async-start | bytes 1216512 | tf_op jit(solution)/shard_map/all_gather | solution.py:124
  7.9 115.9 %all-gather.16.cloned.1.call-start = ((), (), s32[]{:S(2)}) async-start(), calls=%async_computation.9 | async-start | bytes 1216512 | tf_op jit(solution)/shard_map/all_gather | solution.py:126
  8.7 171.2 %all-gather.12.cloned.1.call-start = ((), (), s32[]{:S(2)}) async-start(), calls=%async_computation.7 | async-start | bytes 1216512 | tf_op jit(solution)/shard_map/all_gather | solution.py:127
  9.4 226.4 %all-gather.18.cloned.1.call-start = ((), (), s32[]{:S(2)}) async-start(), calls=%async_computation.10 | async-start | bytes 1216512 | tf_op jit(solution)/shard_map/all_gather | solution.py:129
  10.0 291.2 %all-gather.20.cloned.1.call-start = ((), (), s32[]{:S(2)}) async-start(), calls=%async_computation.11 | async-start | bytes 4866048 | tf_op jit(solution)/shard_map/all_gather | solution.py:133
  10.6 355.9 %all-gather.22.cloned.1.call-start = ((), (), s32[]{:S(2)}) async-start(), calls=%async_computation.12 | async-start | bytes 4866048 | tf_op jit(solution)/shard_map/all_gather | solution.py:135
  11.2 411.2 %all-gather.24.cloned.1.call-start = ((), (), s32[]{:S(2)}) async-start(), calls=%async_computation.13 | async-start | bytes 1216512 | tf_op jit(solution)/shard_map/all_gather | solution.py:139
  11.9 468.0 %all-gather.26.cloned.1.call-start = ((), (), s32[]{:S(2)}) async-start(), calls=%async_computation.18 | async-start | bytes 1622016 | tf_op jit(solution)/shard_map/all_gather | solution.py:266
  66.4 118.5 %copy-start.30 = (pred[7,128,128]{1,2,0:T(8,128)(4,1)}, pred[7,128,128]{1,2,0:T(8,128)(4,1)S(1)}, u32[]{:S(2)}) copy-start(pred[7,128,128]{1,2,0:T(8,128)(4,1)S(1)} %broadcast_compare_fusion) | copy-start | bytes 344068
  253.2 113.3 %copy-start.65 = (f32[768]{0:T(1024)S(1)}, f32[768]{0:T(1024)}, u32[]{:S(2)}) copy-start(f32[768]{0:T(1024)} %convert_element_type.239) | copy-start | bytes 9220
  424.9 112.6 %all-gather.28.cloned.1.call-start = ((), (), s32[]{:S(2)}) async-start(), calls=%async_computation.19 | async-start | bytes 1622016 | tf_op jit(solution)/shard_map/all_gather | solution.py:265
  425.6 353.9 %reduce-scatter.20.cloned.1.call-start = ((), (), s32[]{:S(2)}) async-start(), calls=%async_computation.17 | async-start | bytes 2433024 | tf_op jit(solution)/shard_map/reduce_scatter | solution.py:390
  427.9 97.2 %copy-start.57 = (f32[28]{0:T(128)}, f32[28]{0:T(128)S(1)}, u32[]{:S(2)}) copy-start(f32[28]{0:T(128)S(1)} %div.64) | copy-start | bytes 340
  433.1 107.7 %copy-start.67 = (f32[28]{0:T(128)S(1)}, f32[28]{0:T(128)}, u32[]{:S(2)}) copy-start(f32[28]{0:T(128)} %copy-done.66) | copy-start | bytes 340
  485.2 62.3 %copy-start.32 = (f32[28,896]{1,0:T(8,128)}, f32[28,896]{1,0:T(8,128)S(1)}, u32[]{:S(2)}) copy-start(f32[28,896]{1,0:T(8,128)S(1)} %get-tuple-element.181) | copy-start | bytes 301060
  485.5 62.0 %copy-start.59 = (f32[28]{0:T(128)}, f32[28]{0:T(128)S(1)}, u32[]{:S(2)}) copy-start(f32[28]{0:T(128)S(1)} %get-tuple-element.146) | copy-start | bytes 340
  560.7 218.8 %reduce-scatter.14.cloned.1.call-start = ((), (), s32[]{:S(2)}) async-start(), calls=%async_computation.14 | async-start | bytes 2433024 | tf_op jit(solution)/shard_map/reduce_scatter | solution.py:380
  633.1 234.4 %reduce-scatter.24.cloned.1.call-start = ((), (), s32[]{:S(2)}) async-start(), calls=%async_computation.21 | async-start | bytes 2433024
  662.9 309.3 %reduce-scatter.26.cloned.1.call-start = ((), (), s32[]{:S(2)}) async-start(), calls=%async_computation.22 | async-start | bytes 2433024
  676.5 399.6 %reduce-scatter.22.cloned.1.call-start = ((), (), s32[]{:S(2)}) async-start(), calls=%async_computation.20 | async-start | bytes 2433024
  687.3 530.6 %reduce-scatter.18.cloned.1.call-start = ((), (), s32[]{:S(2)}) async-start(), calls=%async_computation.16 | async-start | bytes 9732096 | tf_op jit(solution)/shard_map/reduce_scatter | solution.py:386
  701.5 657.3 %reduce-scatter.16.cloned.1.call-start = ((), (), s32[]{:S(2)}) async-start(), calls=%async_computation.15 | async-start | bytes 9732096 | tf_op jit(solution)/shard_map/reduce_scatter | solution.py:384
  720.6 53.4 %copy-start.69 = (bf16[768,768]{1,0:T(8,128)(2,1)S(1)}, bf16[768,768]{1,0:T(8,128)(2,1)}, u32[]{:S(2)}) copy-start(bf16[768,768]{1,0:T(8,128)(2,1)} %all-gather.14.cloned.1.call-done) | copy-start | bytes 3538948
  (70 other events, 883.4 us)
Sparse Core Ops, SparseCore 0:
  11.0 56.8 all-gather.13
  70.8 53.0 all-gather.15
  126.8 53.0 all-gather.11
  182.7 53.0 all-gather.17
  238.6 62.5 all-gather.19
  303.9 62.4 all-gather.21
  369.4 52.9 all-gather.23
  425.9 54.0 all-gather.25
  483.4 54.0 all-gather.27
  560.8 97.9 reduce-scatter.19
  665.6 98.0 reduce-scatter.13
  769.4 98.0 reduce-scatter.23
  874.2 98.0 reduce-scatter.25
  978.0 98.0 reduce-scatter.21
  1083.4 134.4 reduce-scatter.17
  1224.3 134.5 reduce-scatter.15
where the time goes:
time: 1380 us; the launch traced here: 1370 us
  waiting for transfers between devices  816 us (59%)
  matrix products  218 us (16%)
  blocking collectives  122 us (9%)
  local copies, waits for them, and re-layouts  95.2 us (7%)
  other arithmetic  94.4 us (7%)
  between operations  18.6 us (1%)
    unnamed x19, waiting for transfers between devices  302 us
    reduce_scatter x1, waiting for transfers between devices, body(): lax.psum_scatter(grad_outer_weight, ('dp', 'fsdp'), scatter_dimension=0,...  142 us
    reduce_scatter x1, waiting for transfers between devices, body(): lax.psum_scatter(grad_inner_weight, ('dp', 'fsdp'), scatter_dimension=0,...  141 us
    dot_general x7, matrix products, matmul(): return jnp.dot(left, right, preferred_element_type=jnp.float32)  87.6 us
    unnamed x2, blocking collectives  81.4 us
    dot_general x9, matrix products, against(): lax.dot_general(left, right, (((1,), (1,)), ((), ())), preferred_element_...  54.4 us
    unnamed x195, local copies, waits for them, and re-layouts  50.1 us
    all_gather x1, waiting for transfers between devices, body(): lax.all_gather(w_inner, ('dp', 'fsdp'), axis=0, tiled=True)  47.9 us
  transfers between devices with their start and end apart: 16, of which 13 were waited for; matrix products, arithmetic and copies ran while one was open for 27% of the time, Pallas kernels for 0%

commit v1 on v0

--- a/solution.py
+++ b/solution.py
@@ -4,7 +4,7 @@
 from jax.sharding import PartitionSpec as P
 
 HEADS = 12
-
+BOTH = ("dp", "fsdp")
 
 precise = lax.Precision.HIGHEST
 keep_scale = 1.0 / 0.9
@@ -60,6 +60,130 @@
     mean_cross = jnp.mean(grad_norm * normed, axis=-1, keepdims=True)
     grad_in = rscale * (grad_norm - mean_grad - normed * mean_cross)
     return (grad_in, jnp.sum(grad_out * normed, axis=(0, 1)), jnp.sum(grad_out, axis=(0, 1)))
+
+
+def paired():
+    return lax.axis_size("dp") == 16 and lax.axis_size("fsdp") == 2
+
+
+def place(z, x, c, y):
+    return ((z * 2 + x) * 2 + c) * 2 + y
+
+
+def pairs(move):
+    every = [(z, x, c, y) for z in range(4) for x in range(2) for c in range(2) for y in range(2)]
+    return [(place(*t), place(*move(*t))) for t in every]
+
+
+def first_pairs():
+    return pairs(lambda z, x, c, y: (z, 1 - x, c, y) if c == 0 else (z, x, c, 1 - y))
+
+
+def second_pairs():
+    return pairs(lambda z, x, c, y: (z, x, c, 1 - y) if c == 0 else (z, 1 - x, c, y))
+
+
+def core_pairs():
+    return pairs(lambda z, x, c, y: (z, x, 1 - c, y))
+
+
+def along_pairs(k):
+    return pairs(lambda z, x, c, y: ((z + k) % 4, x, c, y))
+
+
+def whereabouts():
+    index = lax.axis_index(BOTH)
+    return index // 8, index // 4 % 2, index // 2 % 2, index % 2
+
+
+def spot(x, y, c, p1, p2):
+    on_x = jnp.where(c == 0, p1, p2)
+    on_y = jnp.where(c == 0, p2, p1)
+    return x ^ on_x, y ^ on_y
+
+
+def collect(shard):
+    z, x, c, y = whereabouts()
+    shape = (4,) + shard.shape
+    column = jnp.zeros(shape, shard.dtype)
+    column = lax.dynamic_update_index_in_dim(column, shard, z, 0)
+    for k in (1, 2, 3):
+        come = lax.ppermute(shard, BOTH, along_pairs(k))
+        column = lax.dynamic_update_index_in_dim(column, come, (z - k) % 4, 0)
+    one = lax.ppermute(column, BOTH, first_pairs())
+    pair = jnp.stack([column, one])
+    two = lax.ppermute(pair, BOTH, second_pairs())
+    four = jnp.concatenate([pair, two])
+    other = lax.ppermute(four, BOTH, core_pairs())
+    out = jnp.zeros((4, 2, 2, 2) + shard.shape, shard.dtype)
+    for blocks, core in ((four, c), (other, 1 - c)):
+        for p2 in (0, 1):
+            for p1 in (0, 1):
+                at_x, at_y = spot(x, y, core, p1, p2)
+                block = blocks[2 * p2 + p1][:, None, None, None]
+                out = lax.dynamic_update_slice(out, block, (0, at_x, core, at_y, 0, 0))
+    return out.reshape((32,) + shard.shape)
+
+
+def deliver(whole):
+    z, x, c, y = whereabouts()
+    tail = whole.shape[1:]
+    grid = whole.reshape((4, 2, 2, 2) + tail)
+
+    def blocks(core):
+        picked = []
+        for p2 in (0, 1):
+            for p1 in (0, 1):
+                at_x, at_y = spot(x, y, core, p1, p2)
+                block = lax.dynamic_slice(grid, (0, at_x, core, at_y, 0, 0), (4, 1, 1, 1) + tail)
+                picked.append(block.reshape((4,) + tail))
+        return jnp.stack(picked).reshape((2, 2, 4) + tail)
+
+    def add(kept, come):
+        return (kept.astype(jnp.float32) + come.astype(jnp.float32)).astype(jnp.bfloat16)
+
+    come = lax.ppermute(blocks(1 - c), BOTH, core_pairs())
+    held = add(blocks(c), come)
+    held = add(held[0], lax.ppermute(held[1], BOTH, second_pairs()))
+    held = add(held[0], lax.ppermute(held[1], BOTH, first_pairs()))
+    total = lax.dynamic_index_in_dim(held, z, 0, keepdims=False).astype(jnp.float32)
+    for k in (1, 2, 3):
+        away = lax.dynamic_index_in_dim(held, (z + k) % 4, 0, keepdims=False)
+        total = total + lax.ppermute(away, BOTH, along_pairs(k)).astype(jnp.float32)
+    return total
+
+
+def gather_all(shards):
+    if not paired():
+        return [lax.all_gather(s, BOTH, axis=0, tiled=True) for s in shards]
+    sizes = [s.size for s in shards]
+    flat = jnp.concatenate([s.reshape(-1) for s in shards])
+    rows = -(-flat.size // (768 * 16)) * 16
+    flat = jnp.pad(flat, (0, rows * 768 - flat.size)).reshape(rows, 768)
+    whole = collect(flat).reshape(32, -1)
+    outs, at = [], 0
+    for s, size in zip(shards, sizes):
+        outs.append(whole[:, at : at + size].reshape((32 * s.shape[0],) + s.shape[1:]))
+        at += size
+    return outs
+
+
+def scatter_all(wholes):
+    if not paired():
+        return [lax.psum_scatter(w, BOTH, scatter_dimension=0, tiled=True) for w in wholes]
+    shapes = [(w.shape[0] // 32,) + w.shape[1:] for w in wholes]
+    flat = jnp.concatenate([w.astype(jnp.bfloat16).reshape(32, -1) for w in wholes], axis=1)
+    rows = -(-flat.shape[1] // (768 * 16)) * 16
+    flat = jnp.pad(flat, ((0, 0), (0, rows * 768 - flat.shape[1]))).reshape(32, rows, 768)
+    part = deliver(flat).reshape(-1)
+    outs, at = [], 0
+    for shape in shapes:
+        size = 1
+        for extent in shape:
+            size *= extent
+        outs.append(part[at : at + size].reshape(shape))
+        at += size
+    return outs
 
 
 def anchor_side(anchors, partners, partners_all, flags, column_ok, inv_temp):
@@ -92,6 +216,55 @@
         * flags[:, None]
     )
     return inv_temp * jnp.dot(back_shares, anchors_all.astype(jnp.float32), precision=precise)
+
+
+def every_side(anchors, partners, anchors_all, partners_all, flags, column_ok, inv_temp):
+    sent_slots = anchors.shape[0]
+    held_total = jnp.sum(column_ok)
+    logits = against(anchors_all, partners_all) * inv_temp
+    logits = jnp.where(column_ok[None, :] > 0, logits, -1e30)
+    sim_peak = jnp.max(logits, axis=-1, keepdims=True)
+    sim_total = sim_peak + jnp.log(jnp.sum(jnp.exp(logits - sim_peak), axis=-1, keepdims=True))
+    positive = inv_temp * jnp.sum(
+        anchors_all.astype(jnp.float32) * partners_all.astype(jnp.float32), axis=-1
+    )
+    weights = column_ok / held_total
+    loss = jnp.sum(weights * (sim_total[:, 0] - positive))
+    shares = jnp.exp(logits - sim_total) * weights[:, None]
+    temp_grad = jnp.sum(weights * positive) - jnp.sum(
+        shares * jnp.where(column_ok[None, :] > 0, logits, 0.0)
+    )
+    first_slot = lax.axis_index(BOTH) * sent_slots
+    own_rows = lax.dynamic_slice_in_dim(shares, first_slot, sent_slots, 0)
+    own_columns = lax.dynamic_slice_in_dim(shares, first_slot, sent_slots, 1)
+    own_weight = flags / held_total
+    grad_anchor = inv_temp * (
+        jnp.dot(own_rows, partners_all.astype(jnp.float32), precision=precise)
+        - own_weight[:, None] * partners.astype(jnp.float32)
+    )
+    grad_partner = inv_temp * (
+        lax.dot_general(
+            own_columns,
+            anchors_all.astype(jnp.float32),
+            (((0,), (0,)), ((), ())),
+            precision=precise,
+        )
+        - own_weight[:, None] * anchors.astype(jnp.float32)
+    )
+    return loss, temp_grad, grad_anchor, grad_partner
+
+
+def shared_sides(anchors, partners, anchors_all, partners_all, flags, column_ok, inv_temp):
+    loss_part, temp_part, grad_anchor, sim_total, row_weight, held_total, anchors_f = anchor_side(
+        anchors, partners, partners_all, flags, column_ok, inv_temp
+    )
+    totals_all = lax.all_gather(sim_total, BOTH, axis=0, tiled=True)
+    grad_partner = partner_side(
+        partners, anchors_all, totals_all, column_ok, flags, held_total, inv_temp
+    )
+    grad_partner = grad_partner - inv_temp * row_weight[:, None] * anchors_f
+    loss, temp_grad = lax.psum((loss_part, temp_part), BOTH)
+    return loss, temp_grad, grad_anchor, grad_partner
 
 
 def body(
@@ -120,44 +293,41 @@
     b_pool,
     log_temp,
 ):
-    gathered = (
-        lax.all_gather(w_query, ("dp", "fsdp"), axis=0, tiled=True),
-        lax.all_gather(b_query, ("dp", "fsdp"), axis=0, tiled=True),
-        lax.all_gather(w_key, ("dp", "fsdp"), axis=0, tiled=True),
-        lax.all_gather(w_value, ("dp", "fsdp"), axis=0, tiled=True),
-        lax.all_gather(b_value, ("dp", "fsdp"), axis=0, tiled=True),
-        lax.all_gather(w_attn_out, ("dp", "fsdp"), axis=0, tiled=True),
-        lax.all_gather(b_attn_out, ("dp", "fsdp"), axis=0, tiled=True),
-        lax.all_gather(norm1_gain, ("dp", "fsdp"), axis=0, tiled=True),
-        lax.all_gather(norm1_bias, ("dp", "fsdp"), axis=0, tiled=True),
-        lax.all_gather(w_inner, ("dp", "fsdp"), axis=0, tiled=True),
-        lax.all_gather(b_inner, ("dp", "fsdp"), axis=0, tiled=True),
-        lax.all_gather(w_outer, ("dp", "fsdp"), axis=0, tiled=True),
-        lax.all_gather(b_outer, ("dp", "fsdp"), axis=0, tiled=True),
-        lax.all_gather(norm2_gain, ("dp", "fsdp"), axis=0, tiled=True),
-        lax.all_gather(norm2_bias, ("dp", "fsdp"), axis=0, tiled=True),
-        lax.all_gather(w_pool, ("dp", "fsdp"), axis=0, tiled=True),
-        lax.all_gather(b_pool, ("dp", "fsdp"), axis=0, tiled=True),
-    )
     (
         query_weight,
-        query_bias,
         key_weight,
         value_weight,
+        out_weight,
+        query_bias,
         value_bias,
-        out_weight,
         out_bias,
         gain_one,
         shift_one,
-        inner_weight,
         inner_bias,
-        outer_weight,
         outer_bias,
         gain_two,
         shift_two,
-        pool_weight,
         pool_bias,
-    ) = gathered
+    ) = gather_all(
+        (
+            w_query,
+            w_key,
+            w_value,
+            w_attn_out,
+            b_query,
+            b_value,
+            b_attn_out,
+            norm1_gain,
+            norm1_bias,
+            b_inner,
+            b_outer,
+            norm2_gain,
+            norm2_bias,
+            b_pool,
+        )
+    )
+    (inner_weight,) = gather_all((w_inner,))
+    outer_weight, pool_weight = gather_all((w_outer, w_pool))
     slots, row_len, width = hidden_in.shape
     head_dim = width // HEADS
     tokens = slots * row_len
@@ -223,59 +393,14 @@
     partners = unit_low[sent_slots:]
     flags = held_slots.reshape(sent_slots)
     inv_temp = jnp.exp(-log_temp[0])
-    again = (
-        lax.all_gather(w_query, ("dp", "fsdp"), axis=0, tiled=True),
-        lax.all_gather(b_query, ("dp", "fsdp"), axis=0, tiled=True),
-        lax.all_gather(w_key, ("dp", "fsdp"), axis=0, tiled=True),
-        lax.all_gather(w_value, ("dp", "fsdp"), axis=0, tiled=True),
-        lax.all_gather(b_value, ("dp", "fsdp"), axis=0, tiled=True),
-        lax.all_gather(w_attn_out, ("dp", "fsdp"), axis=0, tiled=True),
-        lax.all_gather(b_attn_out, ("dp", "fsdp"), axis=0, tiled=True),
-        lax.all_gather(norm1_gain, ("dp", "fsdp"), axis=0, tiled=True),
-        lax.all_gather(norm1_bias, ("dp", "fsdp"), axis=0, tiled=True),
-        lax.all_gather(w_inner, ("dp", "fsdp"), axis=0, tiled=True),
-        lax.all_gather(b_inner, ("dp", "fsdp"), axis=0, tiled=True),
-        lax.all_gather(w_outer, ("dp", "fsdp"), axis=0, tiled=True),
-        lax.all_gather(b_outer, ("dp", "fsdp"), axis=0, tiled=True),
-        lax.all_gather(norm2_gain, ("dp", "fsdp"), axis=0, tiled=True),
-        lax.all_gather(norm2_bias, ("dp", "fsdp"), axis=0, tiled=True),
-        lax.all_gather(w_pool, ("dp", "fsdp"), axis=0, tiled=True),
-        lax.all_gather(b_pool, ("dp", "fsdp"), axis=0, tiled=True),
-    )
-    (
-        query_weight,
-        query_bias,
-        key_weight,
-        value_weight,
-        value_bias,
-        out_weight,
-        out_bias,
-        gain_one,
-        shift_one,
-        inner_weight,
-        inner_bias,
-        outer_weight,
-        outer_bias,
-        gain_two,
-        shift_two,
-        pool_weight,
-        pool_bias,
-    ) = again
-    anchors_all, partners_all, flags_all = (
-        lax.all_gather(anchors, ("dp", "fsdp"), axis=0, tiled=True),
-        lax.all_gather(partners, ("dp", "fsdp"), axis=0, tiled=True),
-        lax.all_gather(flags.astype(jnp.bfloat16), ("dp", "fsdp"), axis=0, tiled=True),
+    anchors_all, partners_all, flags_all = gather_all(
+        (anchors, partners, flags.astype(jnp.bfloat16))
     )
     column_ok = flags_all.astype(jnp.float32)
-    loss_part, temp_part, grad_anchor, sim_total, row_weight, held_total, anchors_f = anchor_side(
-        anchors, partners, partners_all, flags, column_ok, inv_temp
-    )
-    totals_all = lax.all_gather(sim_total, ("dp", "fsdp"), axis=0, tiled=True)
-    grad_partner = partner_side(
-        partners, anchors_all, totals_all, column_ok, flags, held_total, inv_temp
-    )
-    grad_partner = grad_partner - inv_temp * row_weight[:, None] * anchors_f
-    totals = lax.psum((loss_part, temp_part), ("dp", "fsdp"))
+    sides = every_side if paired() else shared_sides
+    loss, temp_grad, grad_anchor, grad_partner = sides(
+        anchors, partners, anchors_all, partners_all, flags, column_ok, inv_temp
+    )
     grad_unit = jnp.concatenate([grad_anchor, grad_partner], axis=0)
     grad_pooled = pool_scale * grad_unit - pooled * (
         pool_scale * pool_scale * pool_scale
@@ -371,47 +496,64 @@
         + against(grad_values, value_weight)
     )
     input_grad = input_grad.reshape(slots, row_len, width)
-    shards_out = (
-        lax.psum_scatter(grad_query_weight, ("dp", "fsdp"), scatter_dimension=0, tiled=True),
-        lax.psum_scatter(grad_query_bias, ("dp", "fsdp"), scatter_dimension=0, tiled=True),
-        lax.psum_scatter(grad_key_weight, ("dp", "fsdp"), scatter_dimension=0, tiled=True),
-        lax.psum_scatter(grad_value_weight, ("dp", "fsdp"), scatter_dimension=0, tiled=True),
-        lax.psum_scatter(grad_value_bias, ("dp", "fsdp"), scatter_dimension=0, tiled=True),
-        lax.psum_scatter(grad_out_weight, ("dp", "fsdp"), scatter_dimension=0, tiled=True),
-        lax.psum_scatter(grad_out_bias, ("dp", "fsdp"), scatter_dimension=0, tiled=True),
-        lax.psum_scatter(grad_gain_one, ("dp", "fsdp"), scatter_dimension=0, tiled=True),
-        lax.psum_scatter(grad_shift_one, ("dp", "fsdp"), scatter_dimension=0, tiled=True),
-        lax.psum_scatter(grad_inner_weight, ("dp", "fsdp"), scatter_dimension=0, tiled=True),
-        lax.psum_scatter(grad_inner_bias, ("dp", "fsdp"), scatter_dimension=0, tiled=True),
-        lax.psum_scatter(grad_outer_weight, ("dp", "fsdp"), scatter_dimension=0, tiled=True),
-        lax.psum_scatter(grad_outer_bias, ("dp", "fsdp"), scatter_dimension=0, tiled=True),
-        lax.psum_scatter(grad_gain_two, ("dp", "fsdp"), scatter_dimension=0, tiled=True),
-        lax.psum_scatter(grad_shift_two, ("dp", "fsdp"), scatter_dimension=0, tiled=True),
-        lax.psum_scatter(grad_pool_weight, ("dp", "fsdp"), scatter_dimension=0, tiled=True),
-        lax.psum_scatter(grad_pool_bias, ("dp", "fsdp"), scatter_dimension=0, tiled=True),
+    (part_outer, part_pool, part_gain_two, part_shift_two, part_outer_bias, part_pool_bias) = (
+        scatter_all(
+            (
+                grad_outer_weight,
+                grad_pool_weight,
+                grad_gain_two,
+                grad_shift_two,
+                grad_outer_bias,
+                grad_pool_bias,
+            )
+        )
+    )
+    part_inner, part_inner_bias = scatter_all((grad_inner_weight, grad_inner_bias))
+    (
+        part_query,
+        part_key,
+        part_value,
+        part_out,
+        part_query_bias,
+        part_value_bias,
+        part_out_bias,
+        part_gain_one,
+        part_shift_one,
+    ) = scatter_all(
+        (
+            grad_query_weight,
+            grad_key_weight,
+            grad_value_weight,
+            grad_out_weight,
+            grad_query_bias,
+            grad_value_bias,
+            grad_out_bias,
+            grad_gain_one,
+            grad_shift_one,
+        )
     )
     return (
-        totals[0].reshape(1),
+        loss.reshape(1),
         result,
         input_grad,
-        shards_out[0],
-        shards_out[1],
-        shards_out[2],
-        shards_out[3],
-        shards_out[4],
-        shards_out[5],
-        shards_out[6],
-        shards_out[7],
-        shards_out[8],
-        shards_out[9],
-        shards_out[10],
-        shards_out[11],
-        shards_out[12],
-        shards_out[13],
-        shards_out[14],
-        shards_out[15],
-        shards_out[16],
-        totals[1].reshape(1),
+        part_query,
+        part_query_bias,
+        part_key,
+        part_value,
+        part_value_bias,
+        part_out,
+        part_out_bias,
+        part_gain_one,
+        part_shift_one,
+        part_inner,
+        part_inner_bias,
+        part_outer,
+        part_outer_bias,
+        part_gain_two,
+        part_shift_two,
+        part_pool,
+        part_pool_bias,
+        temp_grad.reshape(1),
     )
 
 

time: 1380 us -> 864 us (0.63)
  waiting for transfers between devices: 816 us -> 131 us
  local copies, waits for them, and re-layouts: 95.2 us -> 290 us
  blocking collectives: 122 us -> 0 us
  starting transfers between devices: 1.42 us -> 76.2 us
  other arithmetic: 94.4 us -> 132 us
    unnamed x19 -> x0, waiting for transfers between devices: 302 us -> none
    reduce_scatter x4 -> x0, waiting for transfers between devices: 283 us -> none  [the longest x1 142 us: body(): lax.psum_scatter(grad_outer_weight, ('dp', 'fsdp'), scatter_dimension=0,...]
    all_gather x9 -> x0, waiting for transfers between devices: 231 us -> none  [the longest x1 47.9 us: body(): lax.all_gather(w_inner, ('dp', 'fsdp'), axis=0, tiled=True)]
    ppermute x0 -> x42, waiting for transfers between devices: none -> 131 us  [the longest x3 48.1 us: deliver(): held = add(held[0], lax.ppermute(held[1], BOTH, second_pairs()))]
    unnamed x2 -> x0, blocking collectives: 81.4 us -> none
    ppermute x0 -> x42, starting transfers between devices: none -> 76.2 us  [the longest x12 25.2 us: collect(): come = lax.ppermute(shard, BOTH, along_pairs(k))]
    reshape x1 -> x38, local copies, waits for them, and re-layouts: 0.07 us -> 61.4 us  [the longest x9 27.3 us: gather_all(): whole[:, at:at + size].reshape((32 * s.shape[0],) + s.shape[1:])]
    dynamic_update_slice x0 -> x48, local copies, waits for them, and re-layouts: none -> 41.1 us  [the longest x32 32.7 us: collect(): out = lax.dynamic_update_slice(out, block, (0, at_x, core, at_y, 0, 0))]
  transfers between devices with their start and end apart: 16 -> 42, of which waited for: 13 -> 19; matrix products, arithmetic and copies ran while one was open for 27% -> 35% of each run, Pallas kernels for 0% -> 0%
where the time goes in v1:
time: 864 us; the launch traced here: 849 us
  local copies, waits for them, and re-layouts  290 us (34%)
  matrix products  212 us (25%)
  other arithmetic  132 us (15%)
  waiting for transfers between devices  131 us (15%)
  starting transfers between devices  76.2 us (9%)
    dot_general x7, matrix products, matmul(): return jnp.dot(left, right, preferred_element_type=jnp.float32)  87.9 us
    unnamed x252, local copies, waits for them, and re-layouts  62.1 us
    dot_general x8, matrix products, against(): lax.dot_general(left, right, (((1,), (1,)), ((), ())), preferred_element_...  53.1 us
    ppermute x3, waiting for transfers between devices, deliver(): held = add(held[0], lax.ppermute(held[1], BOTH, second_pairs()))  48.1 us
    dot_general x7, matrix products, across(): lax.dot_general(left, right, (((0,), (0,)), ((), ())), preferred_element_...  37.5 us
    ppermute x4, waiting for transfers between devices, collect(): one = lax.ppermute(column, BOTH, first_pairs())  32.8 us
    dynamic_update_slice x32, local copies, waits for them, and re-layouts, collect(): out = lax.dynamic_update_slice(out, block, (0, at_x, core, at_y, 0, 0))  32.7 us
    reshape x9, local copies, waits for them, and re-layouts, gather_all(): whole[:, at:at + size].reshape((32 * s.shape[0],) + s.shape[1:])  27.3 us
  transfers between devices with their start and end apart: 42, of which 19 were waited for; matrix products, arithmetic and copies ran while one was open for 35% of the time, Pallas kernels for 0%

profile of v1, /device:TPU:0, one launch (start us, length us, event | category | flops | bytes accessed | tf_op | source)
XLA Modules:
  0.0 849.3 jit_solution(11731623235745875336)
XLA Ops:
  17.4 8.4 concatenate.37
  28.4 9.8 %convert_multiply_fusion = f32[2,2,7,128,768]{4,3,2,1,0:T(8,128)} fusion(s32[2,2,7,128,768]{4,3,2,1,0:T(8,128)} %param.28), kind=kLoop, calls=%fused_computation.29 | loop fusion | flops 5505024 | bytes 22020096 | tf_op jit(solution)/shard_map/mul | solution.py:366
  73.3 6.6 collective-permute-start.1
  94.9 7.8 collective-permute-done.9
  107.9 9.5 %collective-permute-done.3 = bf16[4,112,768]{2,1,0:T(8,128)(2,1)S(1)} collective-permute-done((bf16[4,112,768]{2,1,0:T(8,128)(2,1)S(1)}, bf16[4,112,768]{2,1,0:T(8,128)(2,1)S(1)}, u32[]{:S(2)}, u32[]{:S(2)}) %collective-permute-start.3) | collective-permute-done | bytes 688160 | tf_op jit(solution)/shard_map/ppermute | solution.py:113
  124.9 9.4 %collective-permute-done.15 = bf16[4,128,768]{2,1,0:T(8,128)(2,1)S(1)} collective-permute-done((bf16[4,128,768]{2,1,0:T(8,128)(2,1)S(1)}, bf16[4,128,768]{2,1,0:T(8,128)(2,1)S(1)}, u32[]{:S(2)}, u32[]{:S(2)}) %collective-permute-start.15) | collective-permute-done | bytes 786464 | tf_op jit(solution)/shard_map/ppermute | solution.py:113
  145.6 9.3 %collective-permute-done.16 = bf16[2,4,128,768]{3,2,1,0:T(8,128)(2,1)S(1)} collective-permute-done((bf16[2,4,128,768]{3,2,1,0:T(8,128)(2,1)S(1)}, bf16[2,4,128,768]{3,2,1,0:T(8,128)(2,1)S(1)}, u32[]{:S(2)}, u32[]{:S(2)}) %collective-permute-start.16) | collective-permute-done | bytes 1572896 | tf_op jit(solution)/shard_map/ppermute | solution.py:115
  165.8 8.9 %reshape_reshape_reshape.3 = bf16[768,3072]{1,0:T(8,128)(2,1)} reshape(bf16[4,2,2,2,96,768]{5,4,3,2,1,0:T(8,128)(2,1)} %fusion.119) | data formatting | bytes 9437184 | tf_op jit(solution)/shard_map/reshape;reshape;reshape | solution.py:166
  256.0 56.6 %fusion.2 = (bf16[1792,3072]{1,0:T(8,128)(2,1)}, f32[1792,3072]{1,0:T(8,128)}) fusion(f32[3072]{0:T(1024)S(1)} %reshape.860, bf16[1792,768]{1,0:T(8,128)(2,1)S(1)} %bitcast.663, bf16[768,3072]{1,0:T(8,128)(2,1)} %reshape_reshape_reshape.3), kind=kOutput, calls=%fused_computation.4 | convolution fusion | flops 8819048448 | bytes 40513536 | tf_op jit(solution)/shard_map/dot_general | solution.py:16
  337.2 15.0 %convolution_add_fusion = f32[1792,768]{1,0:T(8,128)} fusion(bf16[1792,3072]{1,0:T(8,128)(2,1)} %get-tuple-element.215, bf16[3072,768]{1,0:T(8,128)(2,1)} %reshape.817, f32[768]{0:T(1024)S(1)} %reshape.861), kind=kOutput, calls=%fused_computation.102 | convolution fusion | flops 8457093120 | bytes 21236736 | tf_op jit(solution)/shard_map/dot_general | solution.py:16
  352.2 7.9 fusion.177
  364.4 11.4 %add_convert_fusion = (bf16[2,7,128,768]{3,2,0,1:T(8,128)(2,1)S(1)}, f32[2,7,128,768]{3,2,0,1:T(8,128)}) fusion(f32[768]{0:T(1024)S(1)} %reshape.863, f32[768]{0:T(1024)S(1)} %reshape.862, f32[2,7,128]{2,0,1:T(2,128)S(1)} %get-tuple-element.202, f32[2,7,128]{2,0,1:T(2,128)S(1)} %get-tuple-element.207, f32[2,7,128,768]{3,2,1,0:T(8,128)} %bitcast.610, ...), kind=kLoop, calls=%fused_computation.87 | loop fusion | flops 17891328 | bytes 30318592 | tf_op jit(solution)/shard_map/convert_element_type | solution.py:376
  401.8 9.8 %collective-permute-done.22 = bf16[2,4,64,768]{3,2,1,0:T(8,128)(2,1)S(1)} collective-permute-done((bf16[2,4,64,768]{3,2,1,0:T(8,128)(2,1)S(1)}, bf16[2,4,64,768]{3,2,1,0:T(8,128)(2,1)S(1)}, u32[]{:S(2)}, u32[]{:S(2)}) %collective-permute-start.22) | collective-permute-done | bytes 786464 | tf_op jit(solution)/shard_map/ppermute | solution.py:115
  419.4 8.8 %reshape.881 = bf16[768,3072,1]{1,0,2:T(8,128)(2,1)} reshape(bf16[4,2,2,2,96,768]{5,4,3,2,1,0:T(8,128)(2,1)} %fusion.119) | data formatting | bytes 9437184 | tf_op jit(solution)/shard_map/reshape;reshape;reshape | solution.py:166
  485.3 8.5 %multiply_reduce_fusion = (bf16[768]{0:T(1024)(128)(2,1)}, f32[2,7,128]{2,0,1:T(2,128)S(1)}, f32[2,7,128]{2,0,1:T(2,128)S(1)}, bf16[768]{0:T(1024)(128)(2,1)}, f32[2,7,128,768]{3,2,0,1:T(8,128)S(1)}) fusion(f32[2,7,128,768]{3,2,0,1:T(8,128)} %get-tuple-element.122, f32[7,128]{1,0:T(8,128)S(1)} %copy-done.93, bf16[2,7,128,768]{3,2,1,0:T(8,128)(2,1)} %param.29, ...), kind=kOutput, calls=%fused_computation.79 | convolution fusion | flops 79824896 | bytes 13958796 | tf_op jit(solution)/shard_map/skl,vskd->vsld/dot_general | solution.py:414
  496.7 12.5 %fusion.174 = (bf16[768]{0:T(1024)(128)(2,1)}, bf16[1792,768]{1,0:T(8,128)(2,1)S(1)}) fusion(f32[1792]{0:T(1024)S(1)} %div.130, f32[1792]{0:T(1024)S(1)} %copy-done.80, f32[1792,768]{1,0:T(8,128)} %convolution_add_fusion, f32[2,1,896,768]{3,2,0,1:T(8,128)} %get-tuple-element.130, f32[768]{0:T(1024)S(1)} %copy-done.63, f32[768]{0:T(1024)S(1)} %copy-done.60, ...), kind=kLoop, calls=%fused_computation.414 | loop fusion | flops 27524352 | bytes 35843584 | tf_op jit(solution)/shard_map/reduce_sum | solution.py:421
  509.2 13.8 %convolution_convert_fusion = bf16[3072,768]{1,0:T(8,128)(2,1)} fusion(bf16[1792,3072]{1,0:T(8,128)(2,1)} %get-tuple-element.215, bf16[1792,768]{1,0:T(8,128)(2,1)S(1)} %get-tuple-element.120), kind=kOutput, calls=%fused_computation.96 | convolution fusion | flops 8458076160 | bytes 18481152 | tf_op jit(solution)/shard_map/dot_general | solution.py:26
  523.1 19.6 %fusion.189 = (bf16[3072]{0:T(1024)(128)(2,1)S(1)}, bf16[1792,3072]{1,0:T(8,128)(2,1)}) fusion(f32[1792,3072]{1,0:T(8,128)} %get-tuple-element.216, f32[3072]{0:T(1024)S(1)} %copy-done.90, bf16[1792,768]{1,0:T(8,128)(2,1)S(1)} %get-tuple-element.120, bf16[3072,768]{1,0:T(8,128)(2,1)S(1)} %bitcast.659), kind=kOutput, calls=%fused_computation.425 | convolution fusion | flops 8521774080 | bytes 40519680 | tf_op jit(solution)/shard_map/dot_general | solution.py:20
  542.7 20.3 %multiply_reduce_fusion.8 = (f32[2,896]{1,0:T(2,128)S(1)}, f32[2,896]{1,0:T(2,128)S(1)}, f32[2,896,768]{2,1,0:T(8,128)}) fusion(f32[768]{0:T(1024)S(1)} %copy-done.60, f32[2,896,768]{2,1,0:T(8,128)} %get-tuple-element.126, f32[2,896]{1,0:T(2,128)S(1)} %get-tuple-element.200, f32[2,896,768]{2,1,0:T(8,128)} %get-tuple-element.124, ...), kind=kOutput, calls=%fused_computation.99 | convolution fusion | flops 8474980352 | bytes 43306496 | tf_op jit(solution)/shard_map/dot_general | solution.py:20
  563.0 8.9 %fusion.106 = (f32[896,768]{1,0:T(8,128)}, bf16[896,768]{1,0:T(8,128)(2,1)S(1)}, bf16[768]{0:T(1024)(128)(2,1)S(1)}, bf16[768]{0:T(1024)(128)(2,1)S(1)}) fusion(f32[2,896,768]{2,1,0:T(8,128)} %get-tuple-element.126, f32[2,896]{1,0:T(2,128)S(1)} %broadcast_multiply_fusion.2, f32[2,896]{1,0:T(2,128)S(1)} %broadcast_multiply_fusion.3, ...), kind=kLoop, calls=%fused_computation.205 | loop fusion | flops 13761024 | bytes 20671488 | tf_op jit(solution)/shard_map/reduce_sum | solution.py:493
  663.5 13.5 %convolution_convert_fusion.1 = bf16[768,3072]{1,0:T(8,128)(2,1)} fusion(bf16[1792,768]{1,0:T(8,128)(2,1)S(1)} %copy-done.40, bf16[1792,3072]{1,0:T(8,128)(2,1)} %get-tuple-element.230), kind=kOutput, calls=%fused_computation.97 | convolution fusion | flops 8458076160 | bytes 18481152 | tf_op jit(solution)/shard_map/dot_general | solution.py:26
  748.2 20.1 %collective-permute-done.25 = bf16[2,4,112,768]{3,2,1,0:T(8,128)(2,1)S(1)} collective-permute-done((bf16[2,4,112,768]{3,2,1,0:T(8,128)(2,1)S(1)}, bf16[2,4,112,768]{3,2,1,0:T(8,128)(2,1)S(1)}, u32[]{:S(2)}, u32[]{:S(2)}) %collective-permute-start.25) | collective-permute-done | bytes 1376288 | tf_op jit(solution)/shard_map/ppermute | solution.py:147
  770.3 22.2 %collective-permute-done.37 = bf16[2,4,128,768]{3,2,1,0:T(8,128)(2,1)S(1)} collective-permute-done((bf16[2,4,128,768]{3,2,1,0:T(8,128)(2,1)S(1)}, bf16[2,4,128,768]{3,2,1,0:T(8,128)(2,1)S(1)}, u32[]{:S(2)}, u32[]{:S(2)}) %collective-permute-start.37) | collective-permute-done | bytes 1572896 | tf_op jit(solution)/shard_map/ppermute | solution.py:147
  838.7 7.1 collective-permute-done.40
  (610 shorter events, 516.2 us)
Async XLA Ops:
  3.4 89.5 %collective-permute-start.12 = (bf16[128,768]{1,0:T(8,128)(2,1)}, bf16[128,768]{1,0:T(8,128)(2,1)}, u32[]{:S(2)}, u32[]{:S(2)}) collective-permute-start(bf16[128,768]{1,0:T(8,128)(2,1)} %reshape.816), channel_id=1, source_target_pairs={{0,8},{1,9},{2,10},{3,11},{4,12},{5,13},{6,14},{7,15},{8,16},{9,17... | collective-permute-start | bytes 589832 | tf_op jit(solution)/shard_map/ppermute | solution.py:111
  6.4 87.5 %collective-permute-start.13 = (bf16[128,768]{1,0:T(8,128)(2,1)}, bf16[128,768]{1,0:T(8,128)(2,1)}, u32[]{:S(2)}, u32[]{:S(2)}) collective-permute-start(bf16[128,768]{1,0:T(8,128)(2,1)} %reshape.816), channel_id=1, source_target_pairs={{0,16},{1,17},{2,18},{3,19},{4,20},{5,21},{6,22},{7,23},{8,24},{9,... | collective-permute-start | bytes 589832 | tf_op jit(solution)/shard_map/ppermute | solution.py:111
  9.0 96.4 %collective-permute-start.14 = (bf16[128,768]{1,0:T(8,128)(2,1)}, bf16[128,768]{1,0:T(8,128)(2,1)}, u32[]{:S(2)}, u32[]{:S(2)}) collective-permute-start(bf16[128,768]{1,0:T(8,128)(2,1)} %reshape.816), channel_id=1, source_target_pairs={{0,24},{1,25},{2,26},{3,27},{4,28},{5,29},{6,30},{7,31},{8,0},{9,1... | collective-permute-start | bytes 589832 | tf_op jit(solution)/shard_map/ppermute | solution.py:111
  12.1 53.9 %collective-permute-start.6 = (bf16[96,768]{1,0:T(8,128)(2,1)}, bf16[96,768]{1,0:T(8,128)(2,1)}, u32[]{:S(2)}, u32[]{:S(2)}) collective-permute-start(bf16[96,768]{1,0:T(8,128)(2,1)} %reshape.813), channel_id=1, source_target_pairs={{0,8},{1,9},{2,10},{3,11},{4,12},{5,13},{6,14},{7,15},{8,16},{9,17... | collective-permute-start | bytes 442376 | tf_op jit(solution)/shard_map/ppermute | solution.py:111
  12.7 57.7 %collective-permute-start.7 = (bf16[96,768]{1,0:T(8,128)(2,1)}, bf16[96,768]{1,0:T(8,128)(2,1)}, u32[]{:S(2)}, u32[]{:S(2)}) collective-permute-start(bf16[96,768]{1,0:T(8,128)(2,1)} %reshape.813), channel_id=1, source_target_pairs={{0,16},{1,17},{2,18},{3,19},{4,20},{5,21},{6,22},{7,23},{8,24},{9,... | collective-permute-start | bytes 442376 | tf_op jit(solution)/shard_map/ppermute | solution.py:111
  91.4 26.0 %collective-permute-start.3 = (bf16[4,112,768]{2,1,0:T(8,128)(2,1)S(1)}, bf16[4,112,768]{2,1,0:T(8,128)(2,1)S(1)}, u32[]{:S(2)}, u32[]{:S(2)}) collective-permute-start(bf16[4,112,768]{2,1,0:T(8,128)(2,1)S(1)} %bitcast_dynamic-update-slice_fusion.11), channel_id=1, source_target_pairs={{0,4},{1,5},{2,3},{3,2},{4,0},{5,1},{6,7},{7,6},{8,12},{9,13},{10,... | collective-permute-start | bytes 2064392 | tf_op jit(solution)/shard_map/ppermute | solution.py:113
  103.8 32.2 %collective-permute-start.10 = (bf16[2,4,96,768]{3,2,1,0:T(8,128)(2,1)S(1)}, bf16[2,4,96,768]{3,2,1,0:T(8,128)(2,1)S(1)}, u32[]{:S(2)}, u32[]{:S(2)}) collective-permute-start(bf16[2,4,96,768]{3,2,1,0:T(8,128)(2,1)S(1)} %pad_maximum_fusion.12), channel_id=1, source_target_pairs={{0,1},{1,0},{2,6},{3,7},{4,5},{5,4},{6,2},{7,3},{8,9},{9,8},{10,14... | collective-permute-start | bytes 3538952 | tf_op jit(solution)/shard_map/ppermute | solution.py:115
  106.4 27.9 %collective-permute-start.15 = (bf16[4,128,768]{2,1,0:T(8,128)(2,1)S(1)}, bf16[4,128,768]{2,1,0:T(8,128)(2,1)S(1)}, u32[]{:S(2)}, u32[]{:S(2)}) collective-permute-start(bf16[4,128,768]{2,1,0:T(8,128)(2,1)S(1)} %bitcast_dynamic-update-slice_fusion.8), channel_id=1, source_target_pairs={{0,4},{1,5},{2,3},{3,2},{4,0},{5,1},{6,7},{7,6},{8,12},{9,13},{10,... | collective-permute-start | bytes 2359304 | tf_op jit(solution)/shard_map/ppermute | solution.py:113
  117.5 20.8 %collective-permute-start.4 = (bf16[2,4,112,768]{3,2,1,0:T(8,128)(2,1)S(1)}, bf16[2,4,112,768]{3,2,1,0:T(8,128)(2,1)S(1)}, u32[]{:S(2)}, u32[]{:S(2)}) collective-permute-start(bf16[2,4,112,768]{3,2,1,0:T(8,128)(2,1)S(1)} %pad_maximum_fusion.11), channel_id=1, source_target_pairs={{0,1},{1,0},{2,6},{3,7},{4,5},{5,4},{6,2},{7,3},{8,9},{9,8},{10,14... | collective-permute-start | bytes 4128776 | tf_op jit(solution)/shard_map/ppermute | solution.py:115
  134.4 20.5 %collective-permute-start.16 = (bf16[2,4,128,768]{3,2,1,0:T(8,128)(2,1)S(1)}, bf16[2,4,128,768]{3,2,1,0:T(8,128)(2,1)S(1)}, u32[]{:S(2)}, u32[]{:S(2)}) collective-permute-start(bf16[2,4,128,768]{3,2,1,0:T(8,128)(2,1)S(1)} %pad_maximum_fusion.9), channel_id=1, source_target_pairs={{0,1},{1,0},{2,6},{3,7},{4,5},{5,4},{6,2},{7,3},{8,9},{9,8},{10,14... | collective-permute-start | bytes 4718600 | tf_op jit(solution)/shard_map/ppermute | solution.py:115
  137.3 25.0 %collective-permute-start.11 = (bf16[4,4,96,768]{3,2,1,0:T(8,128)(2,1)S(1)}, bf16[4,4,96,768]{3,2,1,0:T(8,128)(2,1)S(1)}, u32[]{:S(2)}, u32[]{:S(2)}) collective-permute-start(bf16[4,4,96,768]{3,2,1,0:T(8,128)(2,1)S(1)} %pad_maximum_fusion.8), channel_id=1, source_target_pairs={{0,2},{1,3},{2,0},{3,1},{4,6},{5,7},{6,4},{7,5},{8,10},{9,11},{10,... | collective-permute-start | bytes 7077896 | tf_op jit(solution)/shard_map/ppermute | solution.py:117
  140.2 34.5 %collective-permute-start.5 = (bf16[4,4,112,768]{3,2,1,0:T(8,128)(2,1)}, bf16[4,4,112,768]{3,2,1,0:T(8,128)(2,1)}, u32[]{:S(2)}, u32[]{:S(2)}) collective-permute-start(bf16[4,4,112,768]{3,2,1,0:T(8,128)(2,1)} %pad_maximum_fusion.3), channel_id=1, source_target_pairs={{0,2},{1,3},{2,0},{3,1},{4,6},{5,7},{6,4},{7,5},{8,10},{9,11},{10,... | collective-permute-start | bytes 8257544 | tf_op jit(solution)/shard_map/ppermute | solution.py:117
  156.8 156.1 %collective-permute-start.17 = (bf16[4,4,128,768]{3,2,1,0:T(8,128)(2,1)}, bf16[4,4,128,768]{3,2,1,0:T(8,128)(2,1)}, u32[]{:S(2)}, u32[]{:S(2)}) collective-permute-start(bf16[4,4,128,768]{3,2,1,0:T(8,128)(2,1)} %pad_maximum_fusion), channel_id=1, source_target_pairs={{0,2},{1,3},{2,0},{3,1},{4,6},{5,7},{6,4},{7,5},{8,10},{9,11},{10,... | collective-permute-start | bytes 9437192 | tf_op jit(solution)/shard_map/ppermute | solution.py:117
  413.0 29.7 %collective-permute-start.23 = (bf16[4,4,64,768]{3,2,1,0:T(8,128)(2,1)}, bf16[4,4,64,768]{3,2,1,0:T(8,128)(2,1)}, u32[]{:S(2)}, u32[]{:S(2)}) collective-permute-start(bf16[4,4,64,768]{3,2,1,0:T(8,128)(2,1)} %pad_maximum_fusion.10), channel_id=1, source_target_pairs={{0,2},{1,3},{2,0},{3,1},{4,6},{5,7},{6,4},{7,5},{8,10},{9,11},{10,... | collective-permute-start | bytes 4718600 | tf_op jit(solution)/shard_map/ppermute | solution.py:117
  695.7 29.5 %collective-permute-start.30 = (bf16[2,2,4,112,768]{4,3,2,1,0:T(8,128)(2,1)}, bf16[2,2,4,112,768]{4,3,2,1,0:T(8,128)(2,1)}, u32[]{:S(2)}, u32[]{:S(2)}) collective-permute-start(bf16[2,2,4,112,768]{4,3,2,1,0:T(8,128)(2,1)} %bitcast.153), channel_id=1, source_target_pairs={{0,2},{1,3},{2,0},{3,1},{4,6},{5,7},{6,4},{7,5},{8,10},{9,11},{10,... | collective-permute-start | bytes 8257544 | tf_op jit(solution)/shard_map/ppermute | solution.py:145
  709.8 19.6 %collective-permute-start.24 = (bf16[2,2,4,112,768]{4,3,2,1,0:T(8,128)(2,1)}, bf16[2,2,4,112,768]{4,3,2,1,0:T(8,128)(2,1)}, u32[]{:S(2)}, u32[]{:S(2)}) collective-permute-start(bf16[2,2,4,112,768]{4,3,2,1,0:T(8,128)(2,1)} %bitcast.135), channel_id=1, source_target_pairs={{0,2},{1,3},{2,0},{3,1},{4,6},{5,7},{6,4},{7,5},{8,10},{9,11},{10,... | collective-permute-start | bytes 8257544 | tf_op jit(solution)/shard_map/ppermute | solution.py:145
  731.9 36.4 %collective-permute-start.25 = (bf16[2,4,112,768]{3,2,1,0:T(8,128)(2,1)S(1)}, bf16[2,4,112,768]{3,2,1,0:T(8,128)(2,1)S(1)}, u32[]{:S(2)}, u32[]{:S(2)}) collective-permute-start(bf16[2,4,112,768]{3,2,1,0:T(8,128)(2,1)S(1)} %slice_bitcast_fusion.4), channel_id=1, source_target_pairs={{0,1},{1,0},{2,6},{3,7},{4,5},{5,4},{6,2},{7,3},{8,9},{9,8},{10,14... | collective-permute-start | bytes 4128776 | tf_op jit(solution)/shard_map/ppermute | solution.py:147
  735.7 56.9 %collective-permute-start.37 = (bf16[2,4,128,768]{3,2,1,0:T(8,128)(2,1)S(1)}, bf16[2,4,128,768]{3,2,1,0:T(8,128)(2,1)S(1)}, u32[]{:S(2)}, u32[]{:S(2)}) collective-permute-start(bf16[2,4,128,768]{3,2,1,0:T(8,128)(2,1)S(1)} %slice_bitcast_fusion), channel_id=1, source_target_pairs={{0,1},{1,0},{2,6},{3,7},{4,5},{5,4},{6,2},{7,3},{8,9},{9,8},{10,14... | collective-permute-start | bytes 4718600 | tf_op jit(solution)/shard_map/ppermute | solution.py:147
  746.6 48.9 %collective-permute-start.32 = (bf16[4,112,768]{2,1,0:T(8,128)(2,1)S(1)}, bf16[4,112,768]{2,1,0:T(8,128)(2,1)S(1)}, u32[]{:S(2)}, u32[]{:S(2)}) collective-permute-start(bf16[4,112,768]{2,1,0:T(8,128)(2,1)S(1)} %slice_bitcast_fusion.14), channel_id=1, source_target_pairs={{0,4},{1,5},{2,3},{3,2},{4,0},{5,1},{6,7},{7,6},{8,12},{9,13},{10,... | collective-permute-start | bytes 2064392 | tf_op jit(solution)/shard_map/ppermute | solution.py:148
  768.7 31.2 %collective-permute-start.26 = (bf16[4,112,768]{2,1,0:T(8,128)(2,1)S(1)}, bf16[4,112,768]{2,1,0:T(8,128)(2,1)S(1)}, u32[]{:S(2)}, u32[]{:S(2)}) collective-permute-start(bf16[4,112,768]{2,1,0:T(8,128)(2,1)S(1)} %slice_bitcast_fusion.16), channel_id=1, source_target_pairs={{0,4},{1,5},{2,3},{3,2},{4,0},{5,1},{6,7},{7,6},{8,12},{9,13},{10,... | collective-permute-start | bytes 2064392 | tf_op jit(solution)/shard_map/ppermute | solution.py:148
  793.9 33.7 %collective-permute-start.38 = (bf16[4,128,768]{2,1,0:T(8,128)(2,1)}, bf16[4,128,768]{2,1,0:T(8,128)(2,1)}, u32[]{:S(2)}, u32[]{:S(2)}) collective-permute-start(bf16[4,128,768]{2,1,0:T(8,128)(2,1)} %slice_bitcast_fusion.6), channel_id=1, source_target_pairs={{0,4},{1,5},{2,3},{3,2},{4,0},{5,1},{6,7},{7,6},{8,12},{9,13},{10,... | collective-permute-start | bytes 2359304 | tf_op jit(solution)/shard_map/ppermute | solution.py:148
  798.2 23.5 %collective-permute-start.35 = (bf16[112,768]{1,0:T(8,128)(2,1)S(1)}, bf16[112,768]{1,0:T(8,128)(2,1)S(1)}, u32[]{:S(2)}, u32[]{:S(2)}) collective-permute-start(bf16[112,768]{1,0:T(8,128)(2,1)S(1)} %get-tuple-element.177), channel_id=1, source_target_pairs={{0,24},{1,25},{2,26},{3,27},{4,28},{5,29},{6,30},{7,31},{8,0},{9,1... | collective-permute-start | bytes 516104 | tf_op jit(solution)/shard_map/ppermute | solution.py:152
  800.9 22.3 %collective-permute-start.27 = (bf16[112,768]{1,0:T(8,128)(2,1)}, bf16[112,768]{1,0:T(8,128)(2,1)S(1)}, u32[]{:S(2)}, u32[]{:S(2)}) collective-permute-start(bf16[112,768]{1,0:T(8,128)(2,1)} %get-tuple-element.179), channel_id=1, source_target_pairs={{0,8},{1,9},{2,10},{3,11},{4,12},{5,13},{6,14},{7,15},{8,16},{9,17... | collective-permute-start | bytes 516104 | tf_op jit(solution)/shard_map/ppermute | solution.py:152
  805.0 20.6 %collective-permute-start.28 = (bf16[112,768]{1,0:T(8,128)(2,1)}, bf16[112,768]{1,0:T(8,128)(2,1)}, u32[]{:S(2)}, u32[]{:S(2)}) collective-permute-start(bf16[112,768]{1,0:T(8,128)(2,1)} %get-tuple-element.181), channel_id=1, source_target_pairs={{0,16},{1,17},{2,18},{3,19},{4,20},{5,21},{6,22},{7,23},{8,24},{9,... | collective-permute-start | bytes 516104 | tf_op jit(solution)/shard_map/ppermute | solution.py:152
  (134 other events, 1595.1 us)

commit v2 on v0

v2 whole, which is shorter than its diff:
```python
import functools

import jax
import jax.numpy as jnp
from jax import lax
from jax.experimental import pallas as pl
from jax.experimental.pallas import tpu as pltpu
from jax.sharding import PartitionSpec as P

HEADS = 12
BOTH = ("z", "x", "c", "y")
LOW = jnp.bfloat16
FULL = jnp.float32

precise = lax.Precision.HIGHEST
keep_scale = 1.0 / 0.9
inv_root_two = 0.7071067811865476
inv_root_tau = 0.3989422804014327
eps = 1e-06


def matmul(left, right):
    return lax.dot_general(left, right, (((1,), (0,)), ((), ())), preferred_element_type=FULL)


def against(left, right):
    return lax.dot_general(left, right, (((1,), (1,)), ((), ())), preferred_element_type=FULL)


def across(left, right):
    return lax.dot_general(left, right, (((0,), (0,)), ((), ())), preferred_element_type=FULL)


def paired():
    return tuple(lax.axis_size(axis) for axis in BOTH) == (4, 2, 2, 2)


def place(z, x, c, y):
    return ((z * 2 + x) * 2 + c) * 2 + y


def pairs(move):
    every = [(z, x, c, y) for z in range(4) for x in range(2) for c in range(2) for y in range(2)]
    return [(place(*t), place(*move(*t))) for t in every]


def first_pairs():
    return pairs(lambda z, x, c, y: (z, 1 - x, c, y) if c == 0 else (z, x, c, 1 - y))


def second_pairs():
    return pairs(lambda z, x, c, y: (z, x, c, 1 - y) if c == 0 else (z, 1 - x, c, y))


def across_pairs():
    return pairs(lambda z, x, c, y: (z, 1 - x, c, 1 - y))


def core_pairs():
    return pairs(lambda z, x, c, y: (z, x, 1 - c, y))


def along_pairs(k):
    return pairs(lambda z, x, c, y: ((z + k) % 4, x, c, y))


def whereabouts():
    index = lax.axis_index(BOTH)
    return index // 8, index // 4 % 2, index // 2 % 2, index % 2


def send(block, route):
    return lax.ppermute(block, BOTH, route)


def together(*values):
    return lax.optimization_barrier(values)


def along_z(shard):
    return [send(shard, along_pairs(k)) for k in (1, 2, 3)]


def over_cores(own):
    return [send(block, core_pairs()) for block in own]


def where_from(here, core, p1, p2):
    first_x = core == 0
    on_x = jnp.where(first_x, p1, p2)
    on_y = jnp.where(first_x, p2, p1)
    return here[1] ^ on_x, here[3] ^ on_y


def order_kernel(parts, here_ref, *refs):
    blocks, outs = refs[:8], refs[8:]
    here = [here_ref[i] for i in range(4)]
    total = None
    for i in range(8):
        core = here[2] if i < 4 else 1 - here[2]
        x, y = where_from(here, core, i % 2, i // 2 % 2)
        for k in range(4):
            z = lax.rem(here[0] + 4 - k, 4)
            device = place(z, x, core, y)
            item = 0
            for count, out in zip(parts, outs):
                if count == 0:
                    value = blocks[i][k, item].astype(FULL)
                    total = value if total is None else total + value
                    item += 1
                for n in range(count):
                    out[n, device] = blocks[i][k, item]
                    item += 1
                for n in range(-count):
                    out[device, n] = blocks[i][k, item]
                    item += 1
    for count, out in zip(parts, outs):
        if count == 0:
            out[...] = total


def in_order(here, blocks, parts):
    items, rows, width = blocks[0].shape[1:]
    whole = pl.BlockSpec(memory_space=pltpu.VMEM)
    return call(
        functools.partial(order_kernel, parts),
        "order",
        0,
        128 * items * rows * width,
        out_shape=[
            shaped((rows, width), FULL)
            if count == 0
            else shaped((count, 32, rows, width) if count > 0 else (32, -count, rows, width), LOW)
            for count in parts
        ],
        grid_spec=pltpu.PrefetchScalarGridSpec(
            num_scalar_prefetch=1, grid=(), in_specs=[whole] * 8, out_specs=[whole] * len(parts)
        ),
    )(here, *blocks)


def add_low(left, right):
    return (left.astype(FULL) + right.astype(FULL)).astype(LOW)


def halves_of(kept, come):
    return add_low(kept[2:], come[2:]), add_low(kept[:2], come[:2])


def quarters_of(own, come):
    return add_low(own[1], come[1]), add_low(own[0], come[0])


def quarters(kept, come):
    return add_low(kept[0], come[0]), [add_low(kept[n], come[n]) for n in (1, 2, 3)]


def add_all(own, come):
    return sum([part.astype(FULL) for part in come], own.astype(FULL)).astype(LOW)


def over_z(column):
    z = lax.axis_index("z")
    own = lax.dynamic_index_in_dim(column, z, 0, keepdims=False)
    away = [lax.dynamic_index_in_dim(column, (z + k) % 4, 0, keepdims=False) for k in (1, 2, 3)]
    return [own] + [send(part, along_pairs(k)) for k, part in zip((1, 2, 3), away)]


def finish_kernel(inner, vectors, *refs):
    parts, outs = refs[1:5], refs[5:]
    here_ref = refs[0]
    rows, width = parts[0].shape[1:]

    def total(n):
        return sum(part[n].astype(FULL) for part in parts)

    for n in range(inner):
        outs[0][:, n * width : (n + 1) * width] = total(n)
    outs = outs[1:] if inner else outs
    plain = parts[0].shape[0] - inner - (1 if vectors else 0)
    for n in range(plain):
        outs[n][...] = total(inner + n)
    if vectors:
        index = place(here_ref[0], here_ref[1], here_ref[2], here_ref[3])
        value = total(inner + plain)
        piece = width // 32
        band = outs[plain + 1].shape[1]
        per_row = width // band
        outs[plain][...] = pltpu.roll(value, width - piece * index, 1)[: outs[plain].shape[0], :piece]
        at = lax.broadcasted_iota(jnp.int32, value.shape, 0) == 9 + index // per_row
        line = jnp.sum(jnp.where(at, value, 0.0), axis=0, keepdims=True)
        line = jnp.broadcast_to(line, (8, width))
        line = pltpu.roll(line, width - band * lax.rem(index, per_row), 1)
        outs[plain + 1][...] = line[0:1, :band]


def finish(here, parts, inner=0, vectors=0, band=0):
    items, rows, width = parts[0].shape
    plain = items - inner - (1 if vectors else 0)
    shapes = [(rows, inner * width)] if inner else []
    shapes += [(rows, width)] * plain
    shapes += [(vectors, width // 32), (1, band)] if vectors else []
    return call(
        functools.partial(finish_kernel, inner, vectors),
        "finish",
        0,
        12 * items * rows * width,
        grid_spec=pltpu.PrefetchScalarGridSpec(
            num_scalar_prefetch=1,
            grid=(1,),
            in_specs=[fixed(parts[0].shape)] * 4,
            out_specs=[fixed(shape) for shape in shapes],
        ),
        out_shape=[shaped(shape, FULL) for shape in shapes],
    )(here, *parts)


def layout(row_counts, buckets, lengths, row_len):
    slot_count = buckets.shape[0]
    live_rows = jnp.arange(slot_count, dtype=jnp.int32) < row_counts[0]
    sent_count = jnp.right_shift(jnp.int32(4), buckets)
    slot_ids = jnp.arange(4, dtype=jnp.int32)
    held_slots = (slot_ids[None, :] < sent_count[:, None]) & live_rows[:, None]
    sizes_used = jnp.where(held_slots, lengths, 0)
    finish = jnp.cumsum(sizes_used, axis=1, dtype=jnp.int32)
    starts = finish - sizes_used
    places = jnp.arange(row_len, dtype=jnp.int32)
    segment = jnp.sum((places[None, :, None] >= finish[:, None, :]).astype(jnp.int32), axis=2)
    return segment, starts, held_slots


def pick_table(starts, held_slots, row_len):
    rows = starts.shape[0]
    slot = jnp.arange(64, dtype=jnp.int32)
    view, row, k = slot // 32, slot % 32 // 4, slot % 4
    row = jnp.minimum(row, rows - 1)
    real = slot % 32 < rows * 4
    start = starts[row, k]
    held = held_slots[row, k] & real
    token = jnp.arange(2 * row_len, dtype=jnp.int32)
    hit = held[:, None] & (token[None, :] == (view * row_len + start)[:, None])
    here = jnp.arange(rows, dtype=jnp.int32)[:, None] == row[None, :]
    return (here[:, :, None] & hit[None]).astype(LOW)


def call(kernel, name, flops, moved, room=36, **kwargs):
    return pl.pallas_call(
        kernel,
        name=name,
        compiler_params=pltpu.CompilerParams(vmem_limit_bytes=room * 2**20),
        cost_estimate=pl.CostEstimate(flops=flops, transcendentals=0, bytes_accessed=moved),
        **kwargs,
    )


def scalars_spec():
    return pl.BlockSpec(memory_space=pltpu.SMEM)


def hand_on(here, mark):
    for n in range(4):
        mark[n] = here[n]


def fixed(shape):
    zeros = (0,) * len(shape)
    return pl.BlockSpec(shape, lambda *_: zeros)


def shaped(shape, kind):
    return jax.ShapeDtypeStruct(shape, kind)


def project_kernel(here, x, weight, bias, out, mark):
    hand_on(here, mark)
    out[...] = (matmul(x[...], weight[0]) + bias[0]).astype(LOW)


def project(here, flat, weights, biases):
    tokens, width = flat.shape
    return call(
        project_kernel,
        "project",
        6 * tokens * width * width,
        14 * width * width,
        grid=(3,),
        in_specs=[
            scalars_spec(),
            fixed((tokens, width)),
            pl.BlockSpec((1, width, width), lambda j: (j, 0, 0)),
            pl.BlockSpec((1, 1, width), lambda j: (j, 0, 0)),
        ],
        out_specs=[pl.BlockSpec((tokens, width), lambda j: (0, j)), scalars_spec()],
        out_shape=[shaped((tokens, 3 * width), LOW), shaped((4,), jnp.int32)],
    )(here, flat, weights, biases)


def halves(pair, even):
    zero = jnp.zeros_like(pair)
    return jnp.concatenate([jnp.where(even, pair, zero), jnp.where(even, zero, pair)], axis=0)


def attend_kernel(here, qkv, seg_row, seg_col, out, probs, mark):
    hand_on(here, mark)
    length, width = out.shape
    even = lax.broadcasted_iota(jnp.int32, (length, 128), 1) < 64
    same = seg_col[0] == seg_row[0]
    same = jnp.concatenate([same, same], axis=0)
    for p in range(width // 128):
        at = p * 128
        query = halves(qkv[:, at : at + 128], even)
        key = qkv[:, width + at : width + at + 128]
        value = qkv[:, 2 * width + at : 2 * width + at + 128]
        scores = jnp.where(same, against(query, key) * 0.125, -1e30)
        peak = jnp.max(scores, axis=-1, keepdims=True)
        lifted = jnp.exp(scores - peak)
        share = lifted * (1.0 / jnp.sum(lifted, axis=-1, keepdims=True))
        share = share.astype(LOW)
        probs[0, p] = share
        both = matmul(share, value)
        out[:, at : at + 128] = jnp.where(even, both[:length], both[length:]).astype(LOW)


def attend(here, qkv, segment):
    slots, length = segment.shape
    width = qkv.shape[1] // 3
    pairs_of = width // 128
    return call(
        attend_kernel,
        "attend",
        8 * slots * length * length * width,
        10 * slots * length * width,
        grid=(slots,),
        in_specs=[
            scalars_spec(),
            pl.BlockSpec((length, 3 * width), lambda r: (r, 0)),
            pl.BlockSpec((1, 1, length), lambda r: (r, 0, 0)),
            pl.BlockSpec((1, length, 1), lambda r: (r, 0, 0)),
        ],
        out_specs=[
            pl.BlockSpec((length, width), lambda r: (r, 0)),
            pl.BlockSpec((1, pairs_of, 2 * length, length), lambda r: (r, 0, 0, 0)),
            scalars_spec(),
        ],
        out_shape=[
            shaped((slots * length, width), LOW),
            shaped((slots, pairs_of, 2 * length, length), LOW),
            shaped((4,), jnp.int32),
        ],
    )(here, qkv, segment[:, None, :], segment[:, :, None])


def normal(hidden):
    centre = jnp.mean(hidden, axis=-1, keepdims=True)
    offset = hidden - centre
    spread_of = jnp.mean(offset * offset, axis=-1, keepdims=True)
    rscale = lax.rsqrt(spread_of + eps)
    return offset * rscale, rscale


def normal_back(grad_norm, normed, rscale):
    mean_grad = jnp.mean(grad_norm, axis=-1, keepdims=True)
    mean_cross = jnp.mean(grad_norm * normed, axis=-1, keepdims=True)
    return rscale * (grad_norm - mean_grad - normed * mean_cross)


def gelu_parts(inner):
    phi = 0.5 * (1.0 + lax.erf(inner * inv_root_two))
    return inner * phi, phi + inner * jnp.exp(-0.5 * inner * inner) * inv_root_tau


def inner_kernel(
    starts, held, att, x, keep, w_out, w_inner, small,
    n1, nh1, rs1, active, slope, picked, picked_att, picked_rs, picked_active, picked_slope,
    rows_one, rows_unit, rows_att, rows_scale, near, near_att,
):
    row = pl.program_id(0)
    length, width = att.shape
    branch = matmul(att[...], w_out[...]) + small[2:3]
    base = x[0].astype(FULL)
    keeps = keep[:, 0, 0].astype(FULL) * keep_scale
    first = jnp.concatenate([base + branch * keeps[0], base + branch * keeps[1]], axis=0)
    normed, rscale = normal(first)
    nh1[...] = normed.astype(LOW)
    rs1[...] = rscale
    rows_unit[...] = normed
    rows_scale[...] = jnp.broadcast_to(rscale, rows_scale.shape)
    rows_att[...] = att[...].astype(FULL)
    whole_in = normed * small[3:4] + small[4:5]
    rows_one[...] = whole_in
    inner_in = whole_in.astype(LOW)
    n1[...] = inner_in
    step = 256
    for j in range(w_inner.shape[0]):
        for at in range(0, width, step):
            inner = matmul(inner_in, w_inner[j, :, at : at + step])
            inner = inner + small[9 + j : 10 + j, at : at + step]
            value, grad = gelu_parts(inner)
            active[:, j * width + at : j * width + at + step] = value.astype(LOW)
            slope[:, j * width + at : j * width + at + step] = grad.astype(LOW)

    @pl.when(row == 0)
    def _():
        near[...] = jnp.zeros_like(near)
        near_att[...] = jnp.zeros_like(near_att)
        picked_rs[...] = jnp.zeros_like(picked_rs)

    for k in range(4):
        slot = 4 * row + k

        @pl.when(held[row, k] > 0)
        def _():
            start = starts[row, k]
            near_att[pl.ds(slot, 1)] = rows_att[pl.ds(start, 1)]
            for v in range(2):
                to = pl.ds(32 * v + slot, 1)
                near[0, to] = rows_one[pl.ds(length * v + start, 1)]
                near[1, to] = rows_unit[pl.ds(length * v + start, 1)]
                for n in range(2):
                    near[2 + n, to] = keep[v, n, 0, pl.ds(start, 1)].astype(FULL)
                picked_rs[to] = rows_scale[pl.ds(length * v + start, 1)]

    @pl.when(row == pl.num_programs(0) - 1)
    def _():
        picked[...] = near[...].astype(LOW)
        picked_att[...] = near_att[...].astype(LOW)
        begin = near[0].astype(LOW)
        for j in range(w_inner.shape[0]):
            inner = matmul(begin, w_inner[j]) + small[9 + j : 10 + j]
            value, grad = gelu_parts(inner)
            picked_active[:, j * width : (j + 1) * width] = value.astype(LOW)
            picked_slope[:, j * width : (j + 1) * width] = grad.astype(LOW)


def inner_forward(att, hidden, keep_masks, w_out, w_inner, small, starts, held_slots):
    slots, length, width = hidden.shape
    ff = w_inner.shape[0] * width
    two = 2 * length
    return call(
        inner_kernel,
        "inner_forward",
        2 * slots * two * width * ff,
        slots * two * ff * 5,
        grid_spec=pltpu.PrefetchScalarGridSpec(
            num_scalar_prefetch=2,
            grid=(slots,),
            in_specs=[
                pl.BlockSpec((length, width), lambda r, *_: (r, 0)),
                pl.BlockSpec((1, length, width), lambda r, *_: (r, 0, 0)),
                pl.BlockSpec((2, 2, 1, length, width), lambda r, *_: (0, 0, r, 0, 0)),
                fixed((width, width)),
                fixed(w_inner.shape),
                fixed(small.shape),
            ],
            out_specs=[
                pl.BlockSpec((two, width), lambda r, *_: (r, 0)),
                pl.BlockSpec((two, width), lambda r, *_: (r, 0)),
                pl.BlockSpec((two, 1), lambda r, *_: (r, 0)),
                pl.BlockSpec((two, ff), lambda r, *_: (r, 0)),
                pl.BlockSpec((two, ff), lambda r, *_: (r, 0)),
                fixed((4, 64, width)),
                fixed((32, width)),
                fixed((64, 128)),
                fixed((64, ff)),
                fixed((64, ff)),
            ],
            scratch_shapes=[
                pltpu.VMEM((two, width), FULL),
                pltpu.VMEM((two, width), FULL),
                pltpu.VMEM((length, width), FULL),
                pltpu.VMEM((two, 128), FULL),
                pltpu.VMEM((4, 64, width), FULL),
                pltpu.VMEM((32, width), FULL),
            ],
        ),
        out_shape=[
            shaped((slots * two, width), LOW),
            shaped((slots * two, width), LOW),
            shaped((slots * two, 1), FULL),
            shaped((slots * two, ff), LOW),
            shaped((slots * two, ff), LOW),
            shaped((4, 64, width), LOW),
            shaped((32, width), LOW),
            shaped((64, 128), FULL),
            shaped((64, ff), LOW),
            shaped((64, ff), LOW),
        ],
    )(starts, held_slots.astype(jnp.int32), att, hidden, keep_masks, w_out, w_inner, small)


def start_kernel(active, picked, w_outer, small, w_pool, flags, nh2, rs2, cls, pooled, unit):
    outer = matmul(active[...], w_outer[...]) + small[5:6]
    second = picked[0].astype(FULL) + outer * (picked[3].astype(FULL) * keep_scale)
    normed, rscale = normal(second)
    nh2[...] = normed.astype(LOW)
    rs2[...] = jnp.broadcast_to(rscale, rs2.shape)
    out = (normed * small[6:7] + small[7:8]).astype(LOW)
    cls[...] = out
    squashed = jnp.tanh(matmul(out, w_pool[...]) + small[8:9])
    pooled[...] = squashed
    scale = lax.rsqrt(jnp.sum(squashed * squashed, axis=-1, keepdims=True) + eps)
    ones = (squashed * scale).astype(LOW).astype(FULL)
    slot = lax.broadcasted_iota(jnp.int32, ones.shape, 0)
    unit[0] = jnp.where(slot == 28, flags[...], ones).astype(LOW)


def start_forward(active, picked, w_outer, small, w_pool, flags):
    ff, width = w_outer.shape
    return call(
        start_kernel,
        "start_forward",
        128 * width * ff,
        2 * width * ff,
        out_shape=[
            shaped((64, width), LOW),
            shaped((64, 128), FULL),
            shaped((64, width), LOW),
            shaped((64, width), FULL),
            shaped((1, 64, width), LOW),
        ],
    )(active, picked, w_outer, small, w_pool, flags)


def outer_kernel(here, active, n1, keep, w_outer, small, result, nh2, rs2, mark):
    hand_on(here, mark)
    length = n1.shape[0] // 2
    outer = matmul(active[...], w_outer[...]) + small[5:6]
    keeps = keep[:, 0, 0].astype(FULL) * keep_scale
    keeps = jnp.concatenate([keeps[0], keeps[1]], axis=0)
    second = n1[...].astype(FULL) + outer * keeps
    normed, rscale = normal(second)
    nh2[...] = normed.astype(LOW)
    rs2[...] = rscale
    out = (normed * small[6:7] + small[7:8]).astype(LOW)
    result[0, 0] = out[:length]
    result[1, 0] = out[length:]


def outer_forward(here, active, n1, keep_masks, w_outer, small):
    tokens, ff = active.shape
    width = n1.shape[1]
    slots = keep_masks.shape[2]
    length = keep_masks.shape[3]
    two = 2 * length
    return call(
        outer_kernel,
        "outer_forward",
        2 * tokens * width * ff,
        2 * tokens * ff,
        grid=(slots,),
        in_specs=[
            scalars_spec(),
            pl.BlockSpec((two, ff), lambda r: (r, 0)),
            pl.BlockSpec((two, width), lambda r: (r, 0)),
            pl.BlockSpec((2, 1, 1, length, width), lambda r: (0, 1, r, 0, 0)),
            fixed((ff, width)),
            fixed(small.shape),
        ],
        out_specs=[
            pl.BlockSpec((2, 1, length, width), lambda r: (0, r, 0, 0)),
            pl.BlockSpec((two, width), lambda r: (r, 0)),
            pl.BlockSpec((two, 1), lambda r: (r, 0)),
            scalars_spec(),
        ],
        out_shape=[
            shaped((2, slots, length, width), LOW),
            shaped((tokens, width), LOW),
            shaped((tokens, 1), FULL),
            shaped((4,), jnp.int32),
        ],
    )(here, active, n1, keep_masks, w_outer, small)


def split_matmul(left, right):
    upper = left.astype(LOW)
    lower = (left - upper.astype(FULL)).astype(LOW)
    return matmul(upper, right) + matmul(lower, right)


def pool_back(grad_unit, squashed):
    scale = lax.rsqrt(jnp.sum(squashed * squashed, axis=-1, keepdims=True) + eps)
    grad_pooled = scale * grad_unit - squashed * (scale * scale * scale) * jnp.sum(
        squashed * grad_unit, axis=-1, keepdims=True
    )
    return (grad_pooled * (1.0 - squashed * squashed)).astype(LOW)


def loss_kernel(here_ref, *refs):
    blocks = refs[:8]
    temp, pooled, scalars, grad_pre, anchors, partners, flat, sem = refs[8:]
    here = [here_ref[i] for i in range(4)]
    copies = []
    for i in range(8):
        core = here[2] if i < 4 else 1 - here[2]
        x, y = where_from(here, core, i % 2, i // 2 % 2)
        for k in range(4):
            z = lax.rem(here[0] + 4 - k, 4)
            row = pl.multiple_of(place(z, x, core, y) * 32, 32)
            source = blocks[i].at[k, 0]
            for half, target in ((0, anchors), (1, partners)):
                copies.append(
                    pltpu.make_async_copy(
                        source.at[pl.ds(32 * half, 32)], target.at[pl.ds(row, 32)], sem
                    )
                )
    for copy in copies:
        copy.start()
    for copy in copies:
        copy.wait()
    count = anchors.shape[0]
    groups = count // 32
    inv_temp = jnp.exp(-temp[...])
    all_anchors = anchors[...]
    all_partners = partners[...]
    for d in range(groups):
        flat[d : d + 1] = anchors[d * 32 + 28 : d * 32 + 29, :128].astype(FULL)
    marks = flat[...].astype(LOW)
    slot = lax.broadcasted_iota(jnp.int32, (128, count), 0)
    lane = lax.broadcasted_iota(jnp.int32, (128, count), 1)
    wide = matmul(marks, (slot == lane % 32).astype(LOW))
    group = lax.broadcasted_iota(jnp.int32, (groups, count), 0)
    lane = lax.broadcasted_iota(jnp.int32, (groups, count), 1)
    row_ok = jnp.sum(jnp.where(group == lane // 32, wide, 0.0), axis=0, keepdims=True)
    tall_row = lax.broadcasted_iota(jnp.int32, (count, groups), 0)
    tall_group = lax.broadcasted_iota(jnp.int32, (count, groups), 1)
    tall = matmul((tall_row // 32 == tall_group).astype(LOW), marks)
    tall_row = lax.broadcasted_iota(jnp.int32, (count, 128), 0)
    tall_lane = lax.broadcasted_iota(jnp.int32, (count, 128), 1)
    column_ok = jnp.sum(jnp.where(tall_row % 32 == tall_lane, tall, 0.0), axis=1, keepdims=True)
    total_held = jnp.sum(row_ok, axis=1, keepdims=True)
    weight = row_ok / total_held
    raw = against(all_partners, all_anchors) * inv_temp
    positive = []
    eye = lax.broadcasted_iota(jnp.int32, (128, 128), 0)
    eye = eye == lax.broadcasted_iota(jnp.int32, (128, 128), 1)
    for at in range(0, count, 128):
        block = raw[at : at + 128, at : at + 128]
        positive.append(jnp.sum(jnp.where(eye, block, 0.0), axis=0, keepdims=True))
    positive = jnp.concatenate(positive, axis=1)
    masked = jnp.where(column_ok > 0, raw, -1e30)
    peak = jnp.max(masked, axis=0, keepdims=True)
    lifted = jnp.exp(masked - peak)
    whole = jnp.sum(lifted, axis=0, keepdims=True)
    sim_total = peak + jnp.log(whole)
    crossed = jnp.sum(lifted * masked, axis=0, keepdims=True) / whole
    loss = jnp.sum(weight * (sim_total - positive), axis=1, keepdims=True)
    temp_grad = jnp.sum(weight * (positive - crossed), axis=1, keepdims=True)
    scalars[0:1] = jnp.broadcast_to(loss, (1, 128))
    scalars[1:2] = jnp.broadcast_to(temp_grad, (1, 128))
    mine = place(here[0], here[1], here[2], here[3])
    first = pl.multiple_of(mine * 32, 32)
    my_anchors = anchors[pl.ds(first, 32)]
    my_partners = partners[pl.ds(first, 32)]
    tall_lane = lax.broadcasted_iota(jnp.int32, (32, 128), 1)
    tall_row = lax.broadcasted_iota(jnp.int32, (32, 128), 0)
    my_flags = flat[pl.ds(mine, 1)]
    my_ok = jnp.sum(jnp.where(tall_lane == tall_row, my_flags, 0.0), axis=1, keepdims=True)
    my_weight = my_ok / total_held
    back = against(my_partners, all_anchors) * inv_temp
    back_shares = jnp.exp(jnp.where(my_ok > 0, back, -1e30) - sim_total) * weight
    grad_partner = inv_temp * (
        split_matmul(back_shares, all_anchors) - my_weight * my_anchors.astype(FULL)
    )
    mine_masked = jnp.where(row_ok > 0, against(my_anchors, all_partners) * inv_temp, -1e30)
    peak = jnp.max(mine_masked, axis=1, keepdims=True)
    lifted = jnp.exp(mine_masked - peak)
    my_shares = lifted * (my_weight / jnp.sum(lifted, axis=1, keepdims=True))
    grad_anchor = inv_temp * (
        split_matmul(my_shares, all_partners) - my_weight * my_partners.astype(FULL)
    )
    grad_unit = jnp.concatenate([grad_anchor, grad_partner], axis=0)
    grad_pre[...] = pool_back(grad_unit, pooled[...])


def contrast(here, blocks, log_temp, pooled):
    width = pooled.shape[1]
    count = 32 * 32
    whole = pl.BlockSpec(memory_space=pltpu.VMEM)
    return pl.pallas_call(
        loss_kernel,
        name="contrast",
        grid_spec=pltpu.PrefetchScalarGridSpec(
            num_scalar_prefetch=1,
            grid=(),
            in_specs=[pl.BlockSpec(memory_space=pl.ANY)] * 8 + [whole] * 2,
            out_specs=[whole] * 2,
            scratch_shapes=[
                pltpu.VMEM((count, width), LOW),
                pltpu.VMEM((count, width), LOW),
                pltpu.VMEM((32, 128), FULL),
                pltpu.SemaphoreType.DMA,
            ],
        ),
        out_shape=[shaped((2, 128), FULL), shaped((64, width), LOW)],
        compiler_params=pltpu.CompilerParams(vmem_limit_bytes=36 * 2**20),
        cost_estimate=pl.CostEstimate(
            flops=2 * count * count * width, transcendentals=0, bytes_accessed=4 * count * width
        ),
    )(here, *blocks, log_temp.reshape(1, 1), pooled)


def start_back(grad_out, nh2, rs2, picked, rs1, slope, w_outer, w_inner, w_out, small):
    normed = nh2.astype(FULL)
    second = normal_back(grad_out * small[6:7], normed, rs2)
    outer = (second * (picked[3].astype(FULL) * keep_scale)).astype(LOW)
    width = outer.shape[1]
    wide = w_inner.shape[0]
    inner = []
    grad_normed = second
    for j in range(wide):
        grad_active = against(outer, w_outer[j * width : (j + 1) * width])
        low = (grad_active * slope[:, j * width : (j + 1) * width].astype(FULL)).astype(LOW)
        inner.append(low)
        grad_normed = grad_normed + against(low, w_inner[j])
    unit_one = picked[1].astype(FULL)
    first = normal_back(grad_normed * small[3:4], unit_one, rs1)
    kept = first * (picked[2].astype(FULL) * keep_scale)
    branch = (kept[:32] + kept[32:]).astype(LOW)
    base = first[:32] + first[32:]
    att = against(branch, w_out).astype(LOW)

    def down(value):
        return jnp.sum(value.astype(FULL), axis=0, keepdims=True)

    sums = [
        down(branch),
        down(grad_normed * unit_one),
        down(grad_normed),
        down(outer),
        down(grad_out * normed),
        down(grad_out),
    ]
    return outer, inner, branch, base, att, sums, [down(low) for low in inner]


def start_back_kernel(
    grad_pre, w_pool, nh2, rs2, picked, rs1, slope, small, w_outer_hbm, w_inner_hbm, w_out_hbm,
    outer, inner, branch, base, att, sums, w_outer, w_inner, w_out, sems,
):
    copies = [
        pltpu.make_async_copy(source, target, sems.at[n])
        for n, (source, target) in enumerate(
            ((w_outer_hbm, w_outer), (w_inner_hbm, w_inner), (w_out_hbm, w_out))
        )
    ]
    for copy in copies:
        copy.start()
    grad_out = against(grad_pre[...], w_pool[...])
    for copy in copies:
        copy.wait()
    out = start_back(
        grad_out, nh2[...], rs2[:, :1], picked, rs1[:, :1], slope, w_outer, w_inner, w_out[...],
        small,
    )
    width = outer.shape[1]
    outer[...] = out[0]
    for j, low in enumerate(out[1]):
        inner[:, j * width : (j + 1) * width] = low
    branch[...] = out[2]
    base[...] = out[3]
    att[...] = out[4]
    sums[0:2] = jnp.zeros((2, width), FULL)
    for n, value in enumerate(out[5]):
        sums[2 + n : 3 + n] = value
    sums[8:9] = jnp.sum(grad_pre[...].astype(FULL), axis=0, keepdims=True)
    for j, value in enumerate(out[6]):
        sums[9 + j : 10 + j] = value
    sums[13:24] = jnp.zeros((11, width), FULL)


def start_backward(
    grad_pre, w_pool, nh2, rs2, picked, rs1, slope, small, w_outer, w_inner, w_out
):
    ff, width = w_outer.shape
    whole = pl.BlockSpec(memory_space=pltpu.VMEM)
    outside = pl.BlockSpec(memory_space=pl.ANY)
    return call(
        start_back_kernel,
        "start_backward",
        256 * width * ff,
        4 * width * ff,
        in_specs=[whole] * 8 + [outside] * 3,
        out_shape=[
            shaped((64, width), LOW),
            shaped((64, ff), LOW),
            shaped((32, width), LOW),
            shaped((32, width), FULL),
            shaped((32, width), LOW),
            shaped((24, width), FULL),
        ],
        scratch_shapes=[
            pltpu.VMEM(w_outer.shape, LOW),
            pltpu.VMEM(w_inner.shape, LOW),
            pltpu.VMEM(w_out.shape, LOW),
            pltpu.SemaphoreType.DMA((3,)),
        ],
    )(grad_pre, w_pool, nh2, rs2, picked, rs1, slope, small, w_outer, w_inner, w_out)


def outer_back_kernel(cot, ok, nh2, rs2, keep, small, grad_outer, second, sums):
    row = pl.program_id(0)
    flow = jnp.concatenate([cot[0, 0], cot[1, 0]], axis=0).astype(FULL)
    okay = jnp.concatenate([ok[0], ok[0]], axis=0)
    grad_out = flow * okay
    normed = nh2[...].astype(FULL)
    keeps = keep[:, 0, 0].astype(FULL) * keep_scale
    keeps = jnp.concatenate([keeps[0], keeps[1]], axis=0)
    grad_second = normal_back(grad_out * small[6:7], normed, rs2[...])
    low = (grad_second * keeps).astype(LOW)
    grad_outer[...] = low
    second[...] = grad_second.astype(LOW)

    @pl.when(row == 0)
    def _():
        sums[...] = jnp.zeros_like(sums)

    sums[0:1] += jnp.sum(low.astype(FULL), axis=0, keepdims=True)
    sums[1:2] += jnp.sum(grad_out * normed, axis=0, keepdims=True)
    sums[2:3] += jnp.sum(grad_out, axis=0, keepdims=True)


def outer_backward(cotangent, token_ok, nh2, rs2, keep_masks, small):
    _, slots, length, width = cotangent.shape
    two = 2 * length
    return call(
        outer_back_kernel,
        "outer_backward",
        64 * 2 * slots * two * width,
        18 * slots * two * width // 2,
        grid=(slots,),
        in_specs=[
            pl.BlockSpec((2, 1, length, width), lambda r: (0, r, 0, 0)),
            pl.BlockSpec((1, length, 1), lambda r: (r, 0, 0)),
            pl.BlockSpec((two, width), lambda r: (r, 0)),
            pl.BlockSpec((two, 1), lambda r: (r, 0)),
            pl.BlockSpec((2, 1, 1, length, width), lambda r: (0, 1, r, 0, 0)),
            fixed(small.shape),
        ],
        out_specs=[
            pl.BlockSpec((two, width), lambda r: (r, 0)),
            pl.BlockSpec((two, width), lambda r: (r, 0)),
            fixed((8, width)),
        ],
        out_shape=[
            shaped((slots * two, width), LOW),
            shaped((slots * two, width), LOW),
            shaped((8, width), FULL),
        ],
    )(cotangent, token_ok, nh2, rs2, keep_masks, small)


def inner_back_kernel(
    grad_outer, slope, second, nh1, rs1, keep, w_outer, w_inner, w_out, small,
    grad_inner, grad_branch, grad_att, base, sums, wide_sums,
):
    row = pl.program_id(0)
    length = grad_branch.shape[0]
    width = grad_branch.shape[1]
    step = 256

    @pl.when(row == 0)
    def _():
        sums[...] = jnp.zeros_like(sums)
        wide_sums[...] = jnp.zeros_like(wide_sums)

    low_outer = grad_outer[...]
    grad_normed = second[...].astype(FULL)
    for j in range(w_inner.shape[0]):
        for at in range(0, width, step):
            lane = j * width + at
            grad_active = against(low_outer, w_outer[lane : lane + step])
            low = (grad_active * slope[:, lane : lane + step].astype(FULL)).astype(LOW)
            grad_inner[:, lane : lane + step] = low
            wide_sums[:, lane : lane + step] += jnp.sum(low.astype(FULL), axis=0, keepdims=True)
        grad_normed = grad_normed + against(
            grad_inner[:, j * width : (j + 1) * width], w_inner[j]
        )
    normed = nh1[...].astype(FULL)
    grad_first = normal_back(grad_normed * small[3:4], normed, rs1[...])
    sums[0:1] += jnp.sum(grad_normed * normed, axis=0, keepdims=True)
    sums[1:2] += jnp.sum(grad_normed, axis=0, keepdims=True)
    keeps = keep[:, 0, 0].astype(FULL) * keep_scale
    branch = (grad_first[:length] * keeps[0] + grad_first[length:] * keeps[1]).astype(LOW)
    grad_branch[...] = branch
    sums[2:3] += jnp.sum(branch.astype(FULL), axis=0, keepdims=True)
    base[...] = grad_first[:length] + grad_first[length:]
    grad_att[...] = against(branch, w_out[...]).astype(LOW)


def inner_backward(grad_outer, slope, second, nh1, rs1, keep_masks, w_outer, w_inner, w_out, small):
    tokens, ff = slope.shape
    slots, length, width = keep_masks.shape[2:]
    two = 2 * length
    return call(
        inner_back_kernel,
        "inner_backward",
        4 * tokens * width * ff,
        5 * tokens * ff,
        grid=(slots,),
        in_specs=[
            pl.BlockSpec((two, width), lambda r: (r, 0)),
            pl.BlockSpec((two, ff), lambda r: (r, 0)),
            pl.BlockSpec((two, width), lambda r: (r, 0)),
            pl.BlockSpec((two, width), lambda r: (r, 0)),
            pl.BlockSpec((two, 1), lambda r: (r, 0)),
            pl.BlockSpec((2, 1, 1, length, width), lambda r: (0, 0, r, 0, 0)),
            fixed(w_outer.shape),
            fixed(w_inner.shape),
            fixed(w_out.shape),
            fixed(small.shape),
        ],
        out_specs=[
            pl.BlockSpec((two, ff), lambda r: (r, 0)),
            pl.BlockSpec((length, width), lambda r: (r, 0)),
            pl.BlockSpec((length, width), lambda r: (r, 0)),
            pl.BlockSpec((length, width), lambda r: (r, 0)),
            fixed((8, width)),
            fixed((1, ff)),
        ],
        out_shape=[
            shaped((tokens, ff), LOW),
            shaped((slots * length, width), LOW),
            shaped((slots * length, width), LOW),
            shaped((slots * length, width), FULL),
            shaped((8, width), FULL),
            shaped((1, ff), FULL),
        ],
    )(grad_outer, slope, second, nh1, rs1, keep_masks, w_outer, w_inner, w_out, small)


def attend_back_kernel(grad_att, start_att, table, qkv, probs, grad_qkv, sums):
    row = pl.program_id(0)
    length, width = grad_att.shape
    even = lax.broadcasted_iota(jnp.int32, (length, 128), 1) < 64

    @pl.when(row == 0)
    def _():
        sums[...] = jnp.zeros_like(sums)

    placed = across(table[0, :32, :length], start_att[...])
    whole_att = (grad_att[...].astype(FULL) + placed).astype(LOW)
    for p in range(width // 128):
        at = p * 128
        query = halves(qkv[:, at : at + 128], even)
        key = halves(qkv[:, width + at : width + at + 128], even)
        value = qkv[:, 2 * width + at : 2 * width + at + 128]
        flow = halves(whole_att[:, at : at + 128], even)
        share = probs[0, p]
        share_f = share.astype(FULL)
        grad_share = against(flow, value)
        inside = jnp.sum(grad_share * share_f, axis=-1, keepdims=True)
        grad_scores = (share_f * (grad_share - inside)).astype(LOW)
        grad_value = across(share, flow).astype(LOW)
        side = jnp.concatenate([grad_scores[:length], grad_scores[length:]], axis=1)
        grad_query = (matmul(side, key) * 0.125).astype(LOW)
        grad_key = (across(grad_scores, query) * 0.125).astype(LOW)
        grad_qkv[:, at : at + 128] = grad_query
        grad_qkv[:, width + at : width + at + 128] = grad_key
        grad_qkv[:, 2 * width + at : 2 * width + at + 128] = grad_value
        sums[0:1, at : at + 128] += jnp.sum(grad_query.astype(FULL), axis=0, keepdims=True)
        sums[1:2, at : at + 128] += jnp.sum(grad_value.astype(FULL), axis=0, keepdims=True)


def attend_backward(grad_att, start_att, table, qkv, probs):
    slots, pairs_of, _, length = probs.shape
    width = grad_att.shape[1]
    return call(
        attend_back_kernel,
        "attend_backward",
        16 * slots * length * length * width,
        18 * slots * length * width,
        grid=(slots,),
        in_specs=[
            pl.BlockSpec((length, width), lambda r: (r, 0)),
            fixed((32, width)),
            pl.BlockSpec((1, 64, 2 * length), lambda r: (r, 0, 0)),
            pl.BlockSpec((length, 3 * width), lambda r: (r, 0)),
            pl.BlockSpec((1, pairs_of, 2 * length, length), lambda r: (r, 0, 0, 0)),
        ],
        out_specs=[
            pl.BlockSpec((length, 3 * width), lambda r: (r, 0)),
            fixed((8, width)),
        ],
        out_shape=[shaped((slots * length, 3 * width), LOW), shaped((8, width), FULL)],
    )(grad_att, start_att, table, qkv, probs)


def input_kernel(base, start_base, table, grad_qkv, weights, out):
    width = weights.shape[1]
    total = base[...] + lax.dot_general(
        table[...].astype(FULL),
        start_base[...],
        (((0,), (0,)), ((), ())),
        precision=precise,
        preferred_element_type=FULL,
    )
    for j in range(3):
        total = total + against(grad_qkv[:, j * width : (j + 1) * width], weights[j])
    out[...] = total


def input_gradient(base, start_base, table, grad_qkv, weights):
    tokens, width = base.shape
    rows, _, two = table.shape
    table = table[:, :32, : two // 2].transpose(1, 0, 2).reshape(32, tokens)
    table = jnp.pad(table, ((0, 0), (0, -tokens % 256)))
    step = 256
    return call(
        input_kernel,
        "input_gradient",
        6 * tokens * width * width,
        14 * tokens * width,
        grid=(pl.cdiv(tokens, step),),
        in_specs=[
            pl.BlockSpec((step, width), lambda r: (r, 0)),
            fixed((32, width)),
            pl.BlockSpec((32, step), lambda r: (0, r)),
            pl.BlockSpec((step, 3 * width), lambda r: (r, 0)),
            fixed(weights.shape),
        ],
        out_specs=pl.BlockSpec((step, width), lambda r: (r, 0)),
        out_shape=shaped((tokens, width), FULL),
    )(base, start_base, table, grad_qkv, weights)


def store_part(here, value, z, x, c, y, kept, away, at):
    on_x = here[1] ^ x
    on_y = here[3] ^ y
    index = 2 * on_y + on_x if c == 0 else 2 * on_x + on_y

    @pl.when(here[2] == c)
    def _():
        kept[(index,) + at] = value

    @pl.when(here[2] != c)
    def _():
        away[(index,) + at] = value


def outer_weight_kernel(here_ref, active, grad_outer, start_active, start_outer, kept, away):
    here = [here_ref[i] for i in range(4)]
    rows = kept.shape[3]
    whole = across(active[...], grad_outer[...]) + across(start_active[...], start_outer[...])
    whole = whole.astype(LOW)
    for n in range(8):
        x, c, y = n // 4, n // 2 % 2, n % 2
        store_part(here, whole[n * rows : (n + 1) * rows], 0, x, c, y, kept, away, (0, 0))


def outer_weight(here, active, grad_outer, start_active, start_outer):
    tokens, ff = active.shape
    width = grad_outer.shape[1]
    part = ff // 4
    spec = pl.BlockSpec((4, 1, 1, ff // 32, width), lambda z, _: (0, z, 0, 0, 0))
    shape = shaped((4, 4, 1, ff // 32, width), LOW)
    return call(
        outer_weight_kernel,
        "outer_weight",
        2 * tokens * ff * width,
        2 * tokens * ff,
        grid_spec=pltpu.PrefetchScalarGridSpec(
            num_scalar_prefetch=1,
            grid=(4,),
            in_specs=[
                pl.BlockSpec((tokens, part), lambda z, _: (0, z)),
                pl.BlockSpec((tokens, width), lambda z, _: (0, 0)),
                pl.BlockSpec((64, part), lambda z, _: (0, z)),
                pl.BlockSpec((64, width), lambda z, _: (0, 0)),
            ],
            out_specs=[spec, spec],
        ),
        out_shape=[shape, shape],
    )(here, active, grad_outer, start_active, start_outer)


def store_parts(here, whole, kept, away):
    rows = kept.shape[3]
    for n in range(32):
        z, x, c, y = n // 8, n // 4 % 2, n // 2 % 2, n % 2
        store_part(here, whole[n * rows : (n + 1) * rows], z, x, c, y, kept, away, (z, 0))


def inner_weight_kernel(here_ref, n1, grad_inner, start_n1, start_inner, *refs):
    kept, away = refs[-2:]
    here = [here_ref[i] for i in range(4)]
    step = pl.program_id(0)

    @pl.when(step < 2)
    def _():
        whole = across(n1[...], grad_inner[...]) + across(start_n1[0], start_inner[...])
        store_parts(here, whole.astype(LOW), kept, away)

    if len(refs) > 2:
        att, branch, start_att, start_branch, cls, grad_pre = refs[:6]

        @pl.when(step == 2)
        def _():
            whole = across(att[...], branch[...]) + across(start_att[...], start_branch[...])
            store_parts(here, whole.astype(LOW), kept, away)

        @pl.when(step == 3)
        def _():
            store_parts(here, across(cls[...], grad_pre[...]).astype(LOW), kept, away)


def inner_weight(here, begin, n1, grad_inner, picked, start_inner, *others):
    tokens, _ = grad_inner.shape
    width = n1.shape[1]
    count = 4 if others else 2
    spec = pl.BlockSpec((4, 4, 1, width // 32, width), lambda j, _: (0, 0, j, 0, 0))
    shape = shaped((4, 4, count, width // 32, width), LOW)
    return call(
        inner_weight_kernel,
        "inner_weight",
        4 * tokens * width * width,
        8 * tokens * width,
        grid_spec=pltpu.PrefetchScalarGridSpec(
            num_scalar_prefetch=1,
            grid=(count,),
            in_specs=[
                pl.BlockSpec((tokens, width), lambda j, _: (0, 0)),
                pl.BlockSpec((tokens, width), lambda j, _: (0, begin + jnp.minimum(j, 1))),
                pl.BlockSpec((1, 64, width), lambda j, _: (0, 0, 0)),
                pl.BlockSpec((64, width), lambda j, _: (0, begin + jnp.minimum(j, 1))),
            ]
            + [pl.BlockSpec(other.shape, lambda j, _: (0, 0)) for other in others],
            out_specs=[spec, spec],
        ),
        out_shape=[shape, shape],
    )(here, n1, grad_inner, picked, start_inner, *others)


def attend_weight_kernel(
    here_ref, x, grad_qkv, start_sums, sums_qv, sums_one, sums_two, wide_sums, kept, away
):
    here = [here_ref[i] for i in range(4)]
    step = pl.program_id(0)

    @pl.when(step < 3)
    def _():
        store_parts(here, across(x[...], grad_qkv[...]).astype(LOW), kept, away)

    @pl.when(step == 3)
    def _():
        width = x.shape[1]
        value = start_sums[...] + jnp.concatenate(
            [sums_qv[0:2], sums_one[2:3], sums_one[0:2], sums_two[0:3]]
            + [jnp.zeros((1, width), FULL)]
            + [wide_sums[:, j * width : (j + 1) * width] for j in range(4)]
            + [jnp.zeros((11, width), FULL)],
            axis=0,
        )
        value = value.astype(LOW)
        for index in range(4):
            for z in range(4):
                kept[index, z, 0] = value
                away[index, z, 0] = value


def attend_weight(here, x, grad_qkv, sums):
    tokens, width = x.shape
    spec = pl.BlockSpec((4, 4, 1, width // 32, width), lambda j, _: (0, 0, j, 0, 0))
    shape = shaped((4, 4, 4, width // 32, width), LOW)
    return call(
        attend_weight_kernel,
        "attend_weight",
        6 * tokens * width * width,
        8 * tokens * width,
        grid_spec=pltpu.PrefetchScalarGridSpec(
            num_scalar_prefetch=1,
            grid=(4,),
            in_specs=[
                pl.BlockSpec((tokens, width), lambda j, _: (0, 0)),
                pl.BlockSpec((tokens, width), lambda j, _: (0, jnp.minimum(j, 2))),
            ]
            + [fixed(value.shape) for value in sums],
            out_specs=[spec, spec],
        ),
        out_shape=[shape, shape],
    )(here, x, grad_qkv, *sums)


def gathered(shard):
    return lax.all_gather(shard, BOTH, axis=0, tiled=True)


def scattered(whole):
    return lax.psum_scatter(whole, BOTH, scatter_dimension=0, tiled=True)


def shared_contrast(unit, flags, log_temp, pooled):
    anchors, partners = unit[:28], unit[32:60]
    inv_temp = jnp.exp(-log_temp[0])
    anchors_all, partners_all = gathered(anchors), gathered(partners)
    column_ok = gathered(flags.astype(LOW)).astype(FULL)
    held_total = jnp.sum(column_ok)
    logits = against(anchors, partners_all) * inv_temp
    logits = jnp.where(column_ok[None, :] > 0, logits, -1e30)
    sim_peak = jnp.max(logits, axis=-1, keepdims=True)
    sim_total = sim_peak + jnp.log(jnp.sum(jnp.exp(logits - sim_peak), axis=-1, keepdims=True))
    anchors_f = anchors.astype(FULL)
    partners_f = partners.astype(FULL)
    positive = jnp.sum(anchors_f * partners_f, axis=-1) * inv_temp
    row_weight = flags / held_total
    loss_part = jnp.sum(row_weight * (sim_total[:, 0] - positive))
    shares = jnp.exp(logits - sim_total) * row_weight[:, None]
    temp_part = jnp.sum(row_weight * positive) - jnp.sum(
        shares * jnp.where(column_ok[None, :] > 0, logits, 0.0)
    )
    grad_anchor = inv_temp * (
        jnp.dot(shares, partners_all.astype(FULL), precision=precise)
        - row_weight[:, None] * partners_f
    )
    totals_all = gathered(sim_total[:, 0])
    back = against(partners, anchors_all) * inv_temp
    back = jnp.where(flags[:, None] > 0, back, -1e30)
    back_shares = jnp.exp(back - totals_all[None, :]) * (column_ok / held_total)[None, :]
    grad_partner = inv_temp * (
        jnp.dot(back_shares, anchors_all.astype(FULL), precision=precise)
        - row_weight[:, None] * anchors_f
    )
    loss, temp_grad = lax.psum((loss_part, temp_part), BOTH)
    pad = ((0, 4), (0, 0))
    grad_unit = jnp.concatenate([jnp.pad(grad_anchor, pad), jnp.pad(grad_partner, pad)])
    return loss.reshape(1), temp_grad.reshape(1), pool_back(grad_unit, pooled)


def pack_kernel(here_ref, *refs):
    vectors, b_inner = refs[:9], refs[9]
    w_query, w_key, w_value, w_out, w_inner = refs[10:15]
    one, two, narrow, broad = refs[15:]
    index = place(here_ref[0], here_ref[1], here_ref[2], here_ref[3])
    rows, width = w_query.shape
    band = b_inner.shape[1]
    per_row = width // band
    one[0] = w_query[...]
    one[1] = w_key[...]
    one[2] = w_value[...]
    for j in range(w_inner.shape[1] // width):
        two[j] = w_inner[:, j * width : (j + 1) * width]
    two[4] = w_out[...]
    narrow[...] = jnp.zeros_like(narrow)
    broad[...] = jnp.zeros_like(broad)
    for f, vector in enumerate(vectors):
        narrow[f : f + 1, :rows] = vector[...].astype(FULL)
    broad[0:1, :band] = b_inner[...].astype(FULL)
    placed = pltpu.roll(narrow[...], rows * index, 1)
    line = pltpu.roll(broad[...], band * lax.rem(index, per_row), 1)[0:1]
    at = lax.broadcasted_iota(jnp.int32, placed.shape, 0) == 9 + index // per_row
    placed = jnp.where(at, line, placed)
    one[3] = placed.astype(LOW)


def pack(here, vectors, b_inner, weights):
    w_query, w_key, w_value, w_out, w_inner = weights
    rows, width = w_query.shape
    return call(
        pack_kernel,
        "pack",
        0,
        40 * rows * width,
        room=60,
        grid_spec=pltpu.PrefetchScalarGridSpec(
            num_scalar_prefetch=1,
            grid=(1,),
            in_specs=[fixed((1, rows))] * 9
            + [fixed((1, b_inner.shape[0]))]
            + [fixed(weight.shape) for weight in weights],
            out_specs=[fixed((4, rows, width)), fixed((w_inner.shape[1] // width + 1, rows, width))],
            scratch_shapes=[pltpu.VMEM((24, width), FULL), pltpu.VMEM((8, width), FULL)],
        ),
        out_shape=[
            shaped((4, rows, width), LOW),
            shaped((w_inner.shape[1] // width + 1, rows, width), LOW),
        ],
    )(
        here,
        *[vector[None] for vector in vectors],
        b_inner[None],
        *weights,
    )


def small_sums(start_sums, sums_qv, sums_one, sums_two, wide_sums):
    width = start_sums.shape[1]
    wide = wide_sums.shape[1] // width
    return start_sums + jnp.concatenate(
        [
            sums_qv[0:2],
            sums_one[2:3],
            sums_one[0:2],
            sums_two[0:3],
            jnp.zeros((1, width), FULL),
            wide_sums.reshape(wide, width),
            jnp.zeros((24 - 9 - wide, width), FULL),
        ]
    )


def paired_body(
    hidden_in, row_counts, buckets, lengths, keep_masks, out_cotangent, vectors, b_inner, weights,
    log_temp,
):
    w_query, w_key, w_value, w_attn_out, w_inner, w_outer, w_pool = weights
    slots, length, width = hidden_in.shape
    tokens = slots * length
    ff = w_inner.shape[1]
    wide = ff // width
    index = lax.axis_index(BOTH)
    here = jnp.stack(whereabouts()).astype(jnp.int32)
    flat = hidden_in.reshape(tokens, width)
    first, second = first_pairs(), second_pairs()

    pack_one, pack_two = pack(here, vectors, b_inner, (w_query, w_key, w_value, w_attn_out, w_inner))
    pack_three = jnp.concatenate([w_outer.reshape(wide, -1, width), w_pool[None]])
    come = along_z(pack_one)
    pack_one, pack_two, come = together(pack_one, pack_two, come)

    one = [jnp.stack([pack_one] + come)]
    come = [send(one[0], first), send(one[0], second)]
    come_two = along_z(pack_two)
    one, come, pack_two, come_two = together(one, come, pack_two, come_two)

    one += come
    come = send(one[1], second)
    segment, starts, held_slots = layout(row_counts, buckets, lengths, length)
    token_ok = (segment < 4).astype(FULL)[:, :, None]
    table = pick_table(starts, held_slots, length)
    flags = held_slots.astype(FULL).reshape(slots * 4)
    flag_row = jnp.pad(flags, (0, width - slots * 4))[None]
    two = [jnp.stack([pack_two] + come_two)]
    one, come, two, segment, token_ok, table, flag_row = together(
        one, come, two, segment, token_ok, table, flag_row
    )

    one.append(come)
    one_other = over_cores(one)
    come = [send(two[0], first), send(two[0], second)]
    one, one_other, pack_three = together(one, one_other, pack_three)

    come_three = along_z(pack_three)
    qkv_weights, small = in_order(here, one + one_other, (3, 0))
    qkv_weights = qkv_weights.reshape(3, width, width)
    biases = jnp.stack([small[0], jnp.zeros_like(small[0]), small[1]])[:, None]
    qkv, here = project(here, flat, qkv_weights, biases)
    two, come, pack_three, come_three, here = together(two, come, pack_three, come_three, here)

    two += come
    come = send(two[1], second)
    att, probs, here = attend(here, qkv, segment)
    three = [jnp.stack([pack_three] + come_three)]
    two, come, three, here = together(two, come, three, here)

    two.append(come)
    two_other = over_cores(two)
    come = [send(three[0], first), send(three[0], second), send(three[0], across_pairs())]
    two, two_other, here = together(two, two_other, here)

    inner_weights, out_weight = in_order(here, two + two_other, (wide, 1))
    inner_weights = inner_weights.reshape(wide, width, width)
    out_weight = out_weight.reshape(width, width)
    n1, nh1, rs1, active, slope, picked, picked_att, picked_rs, start_active, start_slope = (
        inner_forward(
            att, hidden_in, keep_masks, out_weight, inner_weights, small, starts, held_slots
        )
    )
    three, come, start_active = together(three, come, start_active)

    three += come
    outer_weights, pool_weight = in_order(here, three + over_cores(three), (-wide, 1))
    outer_weights = outer_weights.reshape(ff, width)
    pool_weight = pool_weight.reshape(width, width)
    start_nh2, start_rs2, cls, pooled, unit = start_forward(
        start_active, picked, outer_weights, small, pool_weight, flag_row
    )
    unit, here = together(unit, here)

    come = along_z(unit)
    result, nh2, rs2, here = outer_forward(here, active, n1, keep_masks, outer_weights, small)
    come, here, token = together(come, here, small)

    own = [jnp.stack([unit] + come)]
    come = [send(own[0], first), send(own[0], second)]
    grad_outer, second_flow, sums_two = outer_backward(
        out_cotangent, token_ok, nh2, rs2, keep_masks, token
    )
    own, come, sums_two = together(own, come, sums_two)

    own += come
    own.append(send(own[1], second))
    scalars, grad_pre = contrast(here, own + over_cores(own), log_temp, pooled)
    loss, temp_grad = scalars[0, :1], scalars[1, :1]
    start_outer, start_inner, start_branch, start_base, start_att, start_sums = start_backward(
        grad_pre, pool_weight, start_nh2, start_rs2, picked, picked_rs, start_slope, small,
        outer_weights, inner_weights, out_weight,
    )

    outer_kept, outer_away = outer_weight(here, active, grad_outer, start_active, start_outer)
    outer_kept, outer_away, token = together(outer_kept, outer_away, small)

    come = send(outer_away, core_pairs())
    grad_inner, grad_branch, grad_att, base, sums_one, wide_sums = inner_backward(
        grad_outer, slope, second_flow, nh1, rs1, keep_masks, outer_weights, inner_weights,
        out_weight, token,
    )
    come, outer_kept, sums_one, start_att = together(come, outer_kept, sums_one, start_att)

    outer_go, outer_own = halves_of(outer_kept, come)
    come = send(outer_go, second)
    grad_qkv, sums_qv = attend_backward(grad_att, start_att, table, qkv, probs)
    outer_own, come, sums_qv = together(outer_own, come, sums_qv)

    outer_go, outer_own = quarters_of(outer_own, come)
    come_outer = send(outer_go, first)
    attend_kept, attend_away = attend_weight(
        here, flat, grad_qkv, (start_sums, sums_qv, sums_one, sums_two, wide_sums)
    )
    outer_own, come_outer, attend_kept, attend_away = together(
        outer_own, come_outer, attend_kept, attend_away
    )

    come = send(attend_away, core_pairs())
    outer_column = add_low(outer_own, come_outer)
    come, attend_kept, outer_column = together(come, attend_kept, outer_column)

    attend_go, attend_own = halves_of(attend_kept, come)
    come = send(attend_go, second)
    attend_go, attend_own, token = together(attend_go, attend_own, here)
    a_kept, a_away = inner_weight(
        token, 0, n1, grad_inner, picked, start_inner, att, grad_branch, picked_att, start_branch,
        cls, grad_pre,
    )
    attend_own, come, a_kept, a_away = together(attend_own, come, a_kept, a_away)

    come_a = send(a_away, core_pairs())
    attend_go, attend_own = quarters_of(attend_own, come)
    come = send(attend_go, first)
    a_kept, come_a, attend_own = together(a_kept, come_a, attend_own)

    a_go, a_own = halves_of(a_kept, come_a)
    come_a = send(a_go, second)
    a_own, token = together(a_own, here)
    b_kept, b_away = inner_weight(token, 2, n1, grad_inner, picked, start_inner)
    come, attend_own, come_a, a_own, b_kept, b_away, outer_column = together(
        come, attend_own, come_a, a_own, b_kept, b_away, outer_column
    )

    come_b = send(b_away, core_pairs())
    a_go, a_own = quarters_of(a_own, come_a)
    come_a = send(a_go, first)
    parts_outer = over_z(outer_column)
    b_kept, come_b, start_base, a_own = together(b_kept, come_b, start_base, a_own)

    b_own, b_go = quarters(b_kept, come_b)
    come_b = [send(part, route) for part, route in zip(b_go, (first, second, across_pairs()))]
    parts_attend = over_z(add_low(attend_own, come))
    input_grad = input_gradient(base, start_base, table, grad_qkv, qkv_weights)
    come_a, a_own, b_own, come_b, parts_attend, parts_outer, token = together(
        come_a, a_own, b_own, come_b, parts_attend, parts_outer, here
    )

    parts_a = over_z(add_low(a_own, come_a))
    b_column = add_all(b_own, come_b)
    (outer_part,) = finish(token, parts_outer)
    query_part, key_part, value_part, own_small, inner_bias_part = finish(
        token, parts_attend, vectors=9, band=b_inner.shape[0]
    )
    parts_b = over_z(b_column)
    inner_a, out_part, pool_part = finish(here, parts_a, inner=2)
    (inner_b,) = finish(here, parts_b, inner=2)
    inner_part = jnp.concatenate([inner_a, inner_b], axis=1)
    input_grad = input_grad.reshape(hidden_in.shape)
    inner_bias_part = inner_bias_part[0]
    parts = [query_part, key_part, value_part, out_part]
    small_parts = [own_small[i] for i in range(9)]
    return (
        loss,
        result,
        input_grad,
        parts[0],
        small_parts[0],
        parts[1],
        parts[2],
        small_parts[1],
        parts[3],
        small_parts[2],
        small_parts[3],
        small_parts[4],
        inner_part,
        inner_bias_part,
        outer_part,
        small_parts[5],
        small_parts[6],
        small_parts[7],
        pool_part,
        small_parts[8],
        temp_grad,
    )


def body(
    hidden_in,
    row_counts,
    buckets,
    lengths,
    keep_masks,
    out_cotangent,
    w_query,
    b_query,
    w_key,
    w_value,
    b_value,
    w_attn_out,
    b_attn_out,
    norm1_gain,
    norm1_bias,
    w_inner,
    b_inner,
    w_outer,
    b_outer,
    norm2_gain,
    norm2_bias,
    w_pool,
    b_pool,
    log_temp,
):
    slots, length, width = hidden_in.shape
    tokens = slots * length
    ff = w_inner.shape[1]
    wide = ff // width
    index = lax.axis_index(BOTH)
    here = jnp.stack(whereabouts()).astype(jnp.int32)
    vectors = (
        b_query,
        b_value,
        b_attn_out,
        norm1_gain,
        norm1_bias,
        b_outer,
        norm2_gain,
        norm2_bias,
        b_pool,
    )
    if paired():
        return paired_body(
            hidden_in, row_counts, buckets, lengths, keep_masks, out_cotangent, vectors, b_inner,
            (w_query, w_key, w_value, w_attn_out, w_inner, w_outer, w_pool), log_temp,
        )
    qkv_weights = jnp.stack([gathered(w) for w in (w_query, w_key, w_value)])
    out_weight = gathered(w_attn_out)
    rows = [gathered(v)[None] for v in vectors]
    rows.append(gathered(b_inner).reshape(wide, width))
    rows.append(jnp.zeros((24 - 9 - wide, width), LOW))
    small = jnp.concatenate(rows).astype(FULL)
    inner_weights = gathered(w_inner).reshape(width, wide, width).transpose(1, 0, 2)
    outer_weights = gathered(w_outer)
    pool_weight = gathered(w_pool)

    segment, starts, held_slots = layout(row_counts, buckets, lengths, length)
    token_ok = (segment < 4).astype(FULL)[:, :, None]
    table = pick_table(starts, held_slots, length)
    flags = held_slots.astype(FULL).reshape(slots * 4)
    flag_row = jnp.pad(flags, (0, width - slots * 4))[None]

    flat = hidden_in.reshape(tokens, width)
    biases = jnp.stack([small[0], jnp.zeros_like(small[0]), small[1]])[:, None]
    qkv, _ = project(here, flat, qkv_weights, biases)
    att, probs, _ = attend(here, qkv, segment)
    n1, nh1, rs1, active, slope, picked, picked_att, picked_rs, start_active, start_slope = (
        inner_forward(
            att, hidden_in, keep_masks, out_weight, inner_weights, small, starts, held_slots
        )
    )
    start_nh2, start_rs2, cls, pooled, unit = start_forward(
        start_active, picked, outer_weights, small, pool_weight, flag_row
    )
    result, nh2, rs2, _ = outer_forward(here, active, n1, keep_masks, outer_weights, small)
    grad_outer, second_flow, sums_two = outer_backward(
        out_cotangent, token_ok, nh2, rs2, keep_masks, small
    )
    loss, temp_grad, grad_pre = shared_contrast(unit[0], flags, log_temp, pooled)
    start_outer, start_inner, start_branch, start_base, start_att, start_sums = start_backward(
        grad_pre, pool_weight, start_nh2, start_rs2, picked, picked_rs, start_slope, small,
        outer_weights, inner_weights, out_weight,
    )
    grad_inner, grad_branch, grad_att, base, sums_one, wide_sums = inner_backward(
        grad_outer, slope, second_flow, nh1, rs1, keep_masks, outer_weights, inner_weights,
        out_weight, small,
    )
    grad_qkv, sums_qv = attend_backward(grad_att, start_att, table, qkv, probs)
    grad_small = small_sums(start_sums, sums_qv, sums_one, sums_two, wide_sums)
    input_grad = input_gradient(base, start_base, table, grad_qkv, qkv_weights)
    input_grad = input_grad.reshape(hidden_in.shape)
    parts = [scattered(across(flat, grad_qkv[:, j * width : (j + 1) * width])) for j in range(3)]
    parts.append(scattered(across(att, grad_branch) + across(picked_att, start_branch)))
    small_parts = [scattered(grad_small[i]) for i in range(9)]
    inner_bias_part = scattered(grad_small[9 : 9 + wide].reshape(ff))
    outer_part = scattered(across(active, grad_outer) + across(start_active, start_outer))
    inner_part = scattered(across(n1, grad_inner) + across(picked[0], start_inner))
    pool_part = scattered(across(cls, grad_pre))
    return (
        loss,
        result,
        input_grad,
        parts[0],
        small_parts[0],
        parts[1],
        parts[2],
        small_parts[1],
        parts[3],
        small_parts[2],
        small_parts[3],
        small_parts[4],
        inner_part,
        inner_bias_part,
        outer_part,
        small_parts[5],
        small_parts[6],
        small_parts[7],
        pool_part,
        small_parts[8],
        temp_grad,
    )


def solution(mesh):
    outer, inner = mesh.shape["dp"], mesh.shape["fsdp"]
    sizes = (4, 2, 2, 2) if (outer, inner) == (16, 2) else (outer, 1, 1, inner)
    mesh = jax.sharding.Mesh(mesh.devices.reshape(sizes), BOTH)
    in_specs = (
        P(BOTH, None, None),
        P(BOTH),
        P(BOTH),
        P(BOTH, None),
        P(None, None, BOTH, None, None),
        P(None, BOTH, None, None),
        P(BOTH, None),
        P(BOTH),
        P(BOTH, None),
        P(BOTH, None),
        P(BOTH),
        P(BOTH, None),
        P(BOTH),
        P(BOTH),
        P(BOTH),
        P(BOTH, None),
        P(BOTH),
        P(BOTH, None),
        P(BOTH),
        P(BOTH),
        P(BOTH),
        P(BOTH, None),
        P(BOTH),
        P(),
    )
    out_specs = (
        P(),
        P(None, BOTH, None, None),
        P(BOTH, None, None),
        P(BOTH, None),
        P(BOTH),
        P(BOTH, None),
        P(BOTH, None),
        P(BOTH),
        P(BOTH, None),
        P(BOTH),
        P(BOTH),
        P(BOTH),
        P(BOTH, None),
        P(BOTH),
        P(BOTH, None),
        P(BOTH),
        P(BOTH),
        P(BOTH),
        P(BOTH, None),
        P(BOTH),
        P(),
    )
    return jax.shard_map(body, mesh=mesh, in_specs=in_specs, out_specs=out_specs, check_vma=False)
```

time: 1380 us -> 402 us (0.29)
  waiting for transfers between devices: 816 us -> 86.4 us
  matrix products: 218 us -> 0 us
  Pallas kernels: 0 us -> 183 us
  blocking collectives: 122 us -> 0 us
  other arithmetic: 94.4 us -> 20.7 us
  starting transfers between devices: 1.42 us -> 73.7 us
  local copies, waits for them, and re-layouts: 95.2 us -> 32.5 us
  between operations: 18.6 us -> 3.11 us
    unnamed x19 -> x0, waiting for transfers between devices: 302 us -> none
    reduce_scatter x4 -> x0, waiting for transfers between devices: 283 us -> none  [the longest x1 142 us: body(): lax.psum_scatter(grad_outer_weight, ('dp', 'fsdp'), scatter_dimension=0,...]
    all_gather x9 -> x0, waiting for transfers between devices: 231 us -> none  [the longest x1 47.9 us: body(): lax.all_gather(w_inner, ('dp', 'fsdp'), axis=0, tiled=True)]
    dot_general x33 -> x0, matrix products: 218 us -> none  [the longest x7 87.6 us: matmul(): return jnp.dot(left, right, preferred_element_type=jnp.float32)]
    pallas_call x0 -> x23, Pallas kernels: none -> 183 us  [the longest x1 30.4 us: inner_backward(): call(inner_back_kernel, 'inner_backward', 4 * tokens * width * ff, 5 * to...]
    ppermute x0 -> x65, waiting for transfers between devices: none -> 86.4 us  [send(): return lax.ppermute(block, BOTH, route)]
    unnamed x2 -> x0, blocking collectives: 81.4 us -> none
    ppermute x0 -> x65, starting transfers between devices: none -> 73.7 us  [send(): return lax.ppermute(block, BOTH, route)]
  transfers between devices with their start and end apart: 16 -> 65, of which waited for: 13 -> 26; matrix products, arithmetic and copies ran while one was open for 27% -> 4% of each run, Pallas kernels for 0% -> 37%
where the time goes in v2:
time: 402 us; the launch traced here: 399 us
  Pallas kernels  183 us (46%)
  waiting for transfers between devices  86.4 us (21%)
  starting transfers between devices  73.7 us (18%)
  local copies, waits for them, and re-layouts  32.5 us (8%)
  other arithmetic  20.7 us (5%)
    ppermute x65, waiting for transfers between devices, send(): return lax.ppermute(block, BOTH, route)  86.4 us
    ppermute x65, starting transfers between devices, send(): return lax.ppermute(block, BOTH, route)  73.7 us
    pallas_call x1, Pallas kernels, inner_backward(): call(inner_back_kernel, 'inner_backward', 4 * tokens * width * ff, 5 * to...  30.4 us
    unnamed x151, local copies, waits for them, and re-layouts  29.1 us
    pallas_call x1, Pallas kernels, inner_forward(): call(inner_kernel, 'inner_forward', 2 * slots * two * width * ff, slots *...  26.5 us
    pallas_call x2, Pallas kernels, inner_weight(): call(inner_weight_kernel, 'inner_weight', 4 * tokens * width * width, 8 *...  19.9 us
    convert_element_type x12, other arithmetic, add_low(): return (left.astype(FULL) + right.astype(FULL)).astype(LOW)  15.1 us
    pallas_call x1, Pallas kernels, outer_weight(): call(outer_weight_kernel, 'outer_weight', 2 * tokens * ff * width, 2 * to...  14.9 us
  transfers between devices with their start and end apart: 65, of which 26 were waited for; matrix products, arithmetic and copies ran while one was open for 4% of the time, Pallas kernels for 37%

profile of v2, /device:TPU:0, one launch (start us, length us, event | category | flops | bytes accessed | tf_op | source)
XLA Modules:
  0.0 399.0 jit_solution(2805622860550132017)
XLA Ops:
  14.1 5.3 %collective-permute-done.1 = bf16[4,24,768]{2,1,0:T(8,128)(2,1)S(1)} collective-permute-done((bf16[4,24,768]{2,1,0:T(8,128)(2,1)}, bf16[4,24,768]{2,1,0:T(8,128)(2,1)S(1)}, u32[]{:S(2)}, u32[]{:S(2)}) %collective-permute-start.1) | collective-permute-done | bytes 147488 | tf_op jit(solution)/shard_map/ppermute | solution.py:73
  35.4 5.7 %collective-permute-done.6 = bf16[5,24,768]{2,1,0:T(8,128)(2,1)S(1)} collective-permute-done((bf16[5,24,768]{2,1,0:T(8,128)(2,1)S(1)}, bf16[5,24,768]{2,1,0:T(8,128)(2,1)S(1)}, u32[]{:S(2)}, u32[]{:S(2)}) %collective-permute-start.6) | collective-permute-done | bytes 184352 | tf_op jit(solution)/shard_map/ppermute | solution.py:73
  42.0 9.2 %collective-permute-done.8.refs_3_ = bf16[4,4,24,768]{3,2,1,0:T(8,128)(2,1)S(1)} collective-permute-done((bf16[4,4,24,768]{3,2,1,0:T(8,128)(2,1)}, bf16[4,4,24,768]{3,2,1,0:T(8,128)(2,1)S(1)}, u32[]{:S(2)}, u32[]{:S(2)}) %collective-permute-start.8) | collective-permute-done | bytes 589856 | tf_op jit(solution)/shard_map/ppermute | solution.py:73
  56.0 4.4 %collective-permute-start.15 = (bf16[5,24,768]{2,1,0:T(8,128)(2,1)S(1)}, bf16[5,24,768]{2,1,0:T(8,128)(2,1)S(1)}, u32[]{:S(2)}, u32[]{:S(2)}) collective-permute-start(bf16[5,24,768]{2,1,0:T(8,128)(2,1)S(1)} %pad_maximum_fusion.5), channel_id=1, source_target_pairs={{0,8},{1,9},{2,10},{3,11},{4,12},{5,13},{6,14},{7,15},{8,16},{9,17... | collective-permute-start | bytes 552968 | tf_op jit(solution)/shard_map/ppermute | solution.py:73
  65.3 5.2 %project.1 = (bf16[896,2304]{1,0:T(8,128)(2,1)S(1)}, s32[4]{0:T(128)S(1)}) custom-call(s32[4]{0:T(128)S(1)} %copy-done.45, bf16[896,768]{1,0:T(8,128)(2,1)S(1)} %bitcast.154, bf16[3,768,768]{2,1,0:T(8,128)(2,1)S(1)} %bitcast.147, f32[3,1,768]{2,1,0:T(1,128)S(1)} %broadcast_in_dim.83.bias), custom_call_target="tpu_custom_call" | custom-call | flops 3170893824 | bytes 8257536 | tf_op jit(solution)/shard_map/project/pallas_call | solution.py:281
  78.2 7.9 %attend.1 = (bf16[896,768]{1,0:T(8,128)(2,1)S(1)}, bf16[7,6,256,128]{3,2,1,0:T(8,128)(2,1)S(1)}, s32[4]{0:T(128)S(1)}) custom-call(s32[4]{0:T(128)S(1)} %get-tuple-element.249.here, bf16[896,2304]{1,0:T(8,128)(2,1)S(1)} %copy-done.2, s32[7,1,128]{2,1,0:T(1,128)S(1)} %broadcast_in_dim.84.seg_row, s32[7,128,1]{2,1,0:T(8,128)S(1)} %copy.70.seg_col), custom_call_target="tpu_custom_call" | custom-call | flops 704643072 | bytes 6881280 | tf_op jit(solution)/shard_map/attend/pallas_call | solution.py:328
  96.8 26.5 %inner_forward.1 = (bf16[1792,768]{1,0:T(8,128)(2,1)S(1)}, bf16[1792,768]{1,0:T(8,128)(2,1)S(1)}, f32[1792,1]{1,0:T(8,128)S(1)}, bf16[1792,3072]{1,0:T(8,128)(2,...) custom-call(s32[7,4]{1,0:T(8,128)S(1)} %fusion.25.starts, ...), custom_call_target="tpu_custom_call" | custom-call | flops 8455716864 | bytes 27525120 | tf_op jit(solution)/shard_map/inner_forward/pallas_call | solution.py:439
  141.1 14.5 %outer_forward.1 = (bf16[2,7,128,768]{3,2,1,0:T(8,128)(2,1)}, bf16[1792,768]{1,0:T(8,128)(2,1)S(1)}, f32[1792,1]{1,0:T(8,128)S(1)}, s32[4]{0:T(128)S(1)}) custom-call(s32[4]{0:T(128)S(1)} %get-tuple-element.283.here_ref.here, bf16[1792,3072]{1,0:T(8,128)(2,1)} %get-tuple-element.284.active, bf16[1792,768]{1,0:T(8,128)(2,1)S(1)} %get-tuple-element.285.n1, ...), custom_call_target="tpu_custom_call" | custom-call | flops 8455716864 | bytes 11010048 | tf_op jit(solution)/shard_map/outer_forward/pallas_call | solution.py:545
  165.8 8.0 %outer_backward.1 = (bf16[1792,768]{1,0:T(8,128)(2,1)S(1)}, bf16[1792,768]{1,0:T(8,128)(2,1)S(1)}, f32[8,768]{1,0:T(8,128)S(1)}) custom-call(bf16[2,7,128,768]{3,2,1,0:T(8,128)(2,1)S(1)} %copy-done.16, f32[7,128,1]{2,1,0:T(8,128)S(1)} %copy.71.ok, bf16[1792,768]{1,0:T(8,128)(2,1)S(1)} %copy-done.18, f32[1792,1]{1,0:T(8,128)S(1)} %copy-done.32, ...), custom_call_target="tpu_custom_call" | custom-call | flops 176160768 | bytes 12386304 | tf_op jit(solution)/shard_map/outer_backward/pallas_call | solution.py:825
  175.8 6.1 %collective-permute-done.35.refs_3_ = bf16[4,1,64,768]{3,2,1,0:T(8,128)(2,1)S(1)} collective-permute-done((bf16[4,1,64,768]{3,2,1,0:T(8,128)(2,1)}, bf16[4,1,64,768]{3,2,1,0:T(8,128)(2,1)S(1)}, u32[]{:S(2)}, u32[]{:S(2)}) %collective-permute-start.35) | collective-permute-done | bytes 393248 | tf_op jit(solution)/shard_map/ppermute | solution.py:73
  183.7 8.9 %contrast.1 = (f32[2,128]{1,0:T(2,128)S(1)}, bf16[64,768]{1,0:T(8,128)(2,1)S(1)}) custom-call(s32[4]{0:T(128)S(1)} %get-tuple-element.378.here_ref.refs_0_, bf16[4,1,64,768]{3,2,1,0:T(8,128)(2,1)} %pad_maximum_fusion.3.refs_0_, bf16[4,1,64,768]{3,2,1,0:T(8,128)(2,1)} %collective-permute-done.33.refs_1_, ...), custom_call_target="tpu_custom_call" | custom-call | flops 1610612736 | bytes 3145728 | tf_op jit(solution)/shard_map/contrast/pallas_call | solution.py:679
  195.6 4.9 %start_backward.1 = (bf16[64,768]{1,0:T(8,128)(2,1)S(1)}, bf16[64,3072]{1,0:T(8,128)(2,1)S(1)}, bf16[32,768]{1,0:T(8,128)(2,1)S(1)}, f32[32,768]{1,0:T(8,128)S(1...) custom-call(bf16[64,768]{1,0:T(8,128)(2,1)S(1)} %get-tuple-element.307.grad_pre.refs_5_, ...), custom_call_target="tpu_custom_call" | custom-call | flops 603979776 | bytes 9437184 | tf_op jit(solution)/shard_map/start_backward/pallas_call | solution.py:777
  201.2 14.9 %outer_weight.1 = (bf16[4,4,1,96,768]{4,3,2,1,0:T(8,128)(2,1)S(1)}, bf16[4,4,1,96,768]{4,3,2,1,0:T(8,128)(2,1)}) custom-call(s32[4]{0:T(128)S(1)} %get-tuple-element.378.here_ref.refs_0_, bf16[1792,3072]{1,0:T(8,128)(2,1)} %get-tuple-element.284.active, bf16[1792,768]{1,0:T(8,128)(2,1)S(1)} %get-tuple-element.302.grad_outer, ...), custom_call_target="tpu_custom_call" | custom-call | flops 8455716864 | bytes 11010048 | tf_op jit(solution)/shard_map/outer_weight/pallas_call | solution.py:1056
  218.8 30.4 %inner_backward.1 = (bf16[1792,3072]{1,0:T(8,128)(2,1)}, bf16[896,768]{1,0:T(8,128)(2,1)S(1)}, bf16[896,768]{1,0:T(8,128)(2,1)S(1)}, f32[896,768]{1,0:T(8,128)S(...) custom-call(bf16[1792,768]{1,0:T(8,128)(2,1)S(1)} %copy-done.49, bf16[1792,3072]{1,0:T(8,128)(2,1)} %get-tuple-element.303.slope, ...), custom_call_target="tpu_custom_call" | custom-call | flops 16911433728 | bytes 27525120 | tf_op jit(solution)/shard_map/inner_backward/pallas_call | solution.py:894
  256.7 13.3 %attend_backward.1 = (bf16[896,2304]{1,0:T(8,128)(2,1)S(1)}, f32[8,768]{1,0:T(8,128)S(1)}) custom-call(bf16[896,768]{1,0:T(8,128)(2,1)S(1)} %copy-done.26, bf16[32,768]{1,0:T(8,128)(2,1)S(1)} %get-tuple-element.324.start_att, bf16[7,64,256]{2,1,0:T(8,128)(2,1)S(1)} %and_convert_fusion.table, bf16[896,2304]{1,0:T(8,128)(2,1)S(1)} %copy-done.3, ...), custom_call_target="tpu_custom_call" | custom-call | flops 1409286144 | bytes 12386304 | tf_op jit(solution)/shard_map/attend_backward/pallas_call | solution.py:967
  274.0 6.6 %attend_weight.1 = (bf16[4,4,4,24,768]{4,3,2,1,0:T(8,128)(2,1)S(1)}, bf16[4,4,4,24,768]{4,3,2,1,0:T(8,128)(2,1)S(1)}) custom-call(s32[4]{0:T(128)S(1)} %get-tuple-element.378.here_ref.refs_0_, bf16[896,768]{1,0:T(8,128)(2,1)S(1)} %bitcast.155, bf16[896,2304]{1,0:T(8,128)(2,1)S(1)} %get-tuple-element.330.grad_qkv, ...), custom_call_target="tpu_custom_call" | custom-call | flops 3170893824 | bytes 5505024 | tf_op jit(solution)/shard_map/attend_weight/pallas_call | solution.py:1164
  288.9 12.0 %inner_weight.2 = (bf16[4,4,4,24,768]{4,3,2,1,0:T(8,128)(2,1)S(1)}, bf16[4,4,4,24,768]{4,3,2,1,0:T(8,128)(2,1)S(1)}) custom-call(s32[4]{0:T(128)S(1)} %get-tuple-element.378.here_ref.refs_0_, bf16[1792,768]{1,0:T(8,128)(2,1)S(1)} %copy-done.11, bf16[1792,3072]{1,0:T(8,128)(2,1)} %get-tuple-element.346.grad_inner, ...), custom_call_target="tpu_custom_call" | custom-call | flops 4227858432 | bytes 11010048 | tf_op jit(solution)/shard_map/inner_weight/pallas_call | solution.py:1112
  312.2 7.8 %inner_weight.3 = (bf16[4,4,2,24,768]{4,3,2,1,0:T(8,128)(2,1)S(1)}, bf16[4,4,2,24,768]{4,3,2,1,0:T(8,128)(2,1)}) custom-call(s32[4]{0:T(128)S(1)} %get-tuple-element.378.here_ref.refs_0_, bf16[1792,768]{1,0:T(8,128)(2,1)S(1)} %copy-done.11, bf16[1792,3072]{1,0:T(8,128)(2,1)S(1)} %bitcast.141, bf16[4,64,768]{2,1,0:T(8,128)(2,1)S(1)} %get-tuple-element.273.picked.start_n1, ...), custom_call_target="tpu_custom_call" | custom-call | flops 4227858432 | bytes 11010048 | tf_op jit(solution)/shard_map/inner_weight/pallas_call | solution.py:1112
  321.0 6.4 %collective-permute-done.45 = bf16[4,4,24,768]{3,2,1,0:T(8,128)(2,1)} collective-permute-done((bf16[4,4,24,768]{3,2,1,0:T(8,128)(2,1)S(1)}, bf16[4,4,24,768]{3,2,1,0:T(8,128)(2,1)}, u32[]{:S(2)}, u32[]{:S(2)}) %collective-permute-start.45) | collective-permute-done | bytes 589856 | tf_op jit(solution)/shard_map/ppermute | solution.py:73
  327.4 5.2 %collective-permute-done.47 = bf16[2,4,4,24,768]{4,3,2,1,0:T(8,128)(2,1)} collective-permute-done((bf16[2,4,4,24,768]{4,3,2,1,0:T(8,128)(2,1)S(1)}, bf16[2,4,4,24,768]{4,3,2,1,0:T(8,128)(2,1)}, u32[]{:S(2)}, u32[]{:S(2)}) %collective-permute-start.47) | collective-permute-done | bytes 1179680 | tf_op jit(solution)/shard_map/ppermute | solution.py:73
  349.8 5.8 %collective-permute-start.58 = (bf16[1,96,768]{2,1,0:T(8,128)(2,1)S(1)}, bf16[1,96,768]{2,1,0:T(8,128)(2,1)S(1)}, u32[]{:S(2)}, u32[]{:S(2)}) collective-permute-start(bf16[1,96,768]{2,1,0:T(8,128)(2,1)S(1)} %get-tuple-element.417), channel_id=1, source_target_pairs={{0,24},{1,25},{2,26},{3,27},{4,28},{5,29},{6,30},{7,31},{8,0},{9,1... | collective-permute-start | bytes 442376 | tf_op jit(solution)/shard_map/ppermute | solution.py:73
  357.5 4.4 %collective-permute-done.57.refs_3_ = bf16[1,96,768]{2,1,0:T(8,128)(2,1)S(1)} collective-permute-done((bf16[1,96,768]{2,1,0:T(8,128)(2,1)S(1)}, bf16[1,96,768]{2,1,0:T(8,128)(2,1)S(1)}, u32[]{:S(2)}, u32[]{:S(2)}) %collective-permute-start.57) | collective-permute-done | bytes 147488 | tf_op jit(solution)/shard_map/ppermute | solution.py:73
  363.4 7.8 %input_gradient.1 = f32[896,768]{1,0:T(8,128)} custom-call(f32[896,768]{1,0:T(8,128)S(1)} %copy-done.13, f32[32,768]{1,0:T(8,128)S(1)} %get-tuple-element.371.start_base, bf16[32,1024]{1,0:T(8,128)(2,1)S(1)} %pad.10.table, bf16[896,2304]{1,0:T(8,128)(2,1)S(1)} %copy-done.7, bf16[3,768,768]{2,1,0:T(8,128)(2,1)S(1)} %bitcast.148), custom_call_target="tpu_custom_call" | custom-call | flops 3170893824 | bytes 9633792 | tf_op jit(solution)/shard_map/input_gradient/pallas_call | solution.py:1008
  385.8 10.5 %collective-permute-done.63.refs_3_ = bf16[2,24,768]{2,1,0:T(8,128)(2,1)S(1)} collective-permute-done((bf16[2,24,768]{2,1,0:T(8,128)(2,1)S(1)}, bf16[2,24,768]{2,1,0:T(8,128)(2,1)S(1)}, u32[]{:S(2)}, u32[]{:S(2)}) %collective-permute-start.63) | collective-permute-done | bytes 73760 | tf_op jit(solution)/shard_map/ppermute | solution.py:73
  (336 shorter events, 164.2 us)
Async XLA Ops:
  20.4 20.7 %collective-permute-start.3 = (bf16[4,4,24,768]{3,2,1,0:T(8,128)(2,1)S(1)}, bf16[4,4,24,768]{3,2,1,0:T(8,128)(2,1)}, u32[]{:S(2)}, u32[]{:S(2)}) collective-permute-start(bf16[4,4,24,768]{3,2,1,0:T(8,128)(2,1)S(1)} %pad_maximum_fusion.2.refs_0_), channel_id=1, source_target_pairs={{0,4},{1,5},{2,3},{3,2},{4,0},{5,1},{6,7},{7,6},{8,12},{9,13},{10,... | collective-permute-start | bytes 1769480 | tf_op jit(solution)/shard_map/ppermute | solution.py:73
  21.9 19.2 %collective-permute-start.4 = (bf16[4,4,24,768]{3,2,1,0:T(8,128)(2,1)S(1)}, bf16[4,4,24,768]{3,2,1,0:T(8,128)(2,1)}, u32[]{:S(2)}, u32[]{:S(2)}) collective-permute-start(bf16[4,4,24,768]{3,2,1,0:T(8,128)(2,1)S(1)} %pad_maximum_fusion.2.refs_0_), channel_id=1, source_target_pairs={{0,1},{1,0},{2,6},{3,7},{4,5},{5,4},{6,2},{7,3},{8,9},{9,8},{10,14... | collective-permute-start | bytes 1769480 | tf_op jit(solution)/shard_map/ppermute | solution.py:73
  52.4 20.1 %collective-permute-start.9 = (bf16[4,5,24,768]{3,2,1,0:T(8,128)(2,1)S(1)}, bf16[4,5,24,768]{3,2,1,0:T(8,128)(2,1)S(1)}, u32[]{:S(2)}, u32[]{:S(2)}) collective-permute-start(bf16[4,5,24,768]{3,2,1,0:T(8,128)(2,1)S(1)} %pad_maximum_fusion.refs_0_), channel_id=1, source_target_pairs={{0,4},{1,5},{2,3},{3,2},{4,0},{5,1},{6,7},{7,6},{8,12},{9,13},{10,... | collective-permute-start | bytes 2211848 | tf_op jit(solution)/shard_map/ppermute | solution.py:73
  54.1 18.5 %collective-permute-start.10 = (bf16[4,5,24,768]{3,2,1,0:T(8,128)(2,1)S(1)}, bf16[4,5,24,768]{3,2,1,0:T(8,128)(2,1)S(1)}, u32[]{:S(2)}, u32[]{:S(2)}) collective-permute-start(bf16[4,5,24,768]{3,2,1,0:T(8,128)(2,1)S(1)} %pad_maximum_fusion.refs_0_), channel_id=1, source_target_pairs={{0,1},{1,0},{2,6},{3,7},{4,5},{5,4},{6,2},{7,3},{8,9},{9,8},{10,14... | collective-permute-start | bytes 2211848 | tf_op jit(solution)/shard_map/ppermute | solution.py:73
  56.0 16.5 %collective-permute-start.15 = (bf16[5,24,768]{2,1,0:T(8,128)(2,1)S(1)}, bf16[5,24,768]{2,1,0:T(8,128)(2,1)S(1)}, u32[]{:S(2)}, u32[]{:S(2)}) collective-permute-start(bf16[5,24,768]{2,1,0:T(8,128)(2,1)S(1)} %pad_maximum_fusion.5), channel_id=1, source_target_pairs={{0,8},{1,9},{2,10},{3,11},{4,12},{5,13},{6,14},{7,15},{8,16},{9,17... | collective-permute-start | bytes 552968 | tf_op jit(solution)/shard_map/ppermute | solution.py:73
  88.9 36.8 %collective-permute-start.19 = (bf16[4,5,24,768]{3,2,1,0:T(8,128)(2,1)S(1)}, bf16[4,5,24,768]{3,2,1,0:T(8,128)(2,1)S(1)}, u32[]{:S(2)}, u32[]{:S(2)}) collective-permute-start(bf16[4,5,24,768]{3,2,1,0:T(8,128)(2,1)S(1)} %pad_maximum_fusion.1.refs_0_), channel_id=1, source_target_pairs={{0,4},{1,5},{2,3},{3,2},{4,0},{5,1},{6,7},{7,6},{8,12},{9,13},{10,... | collective-permute-start | bytes 2211848 | tf_op jit(solution)/shard_map/ppermute | solution.py:73
  90.1 35.6 %collective-permute-start.20 = (bf16[4,5,24,768]{3,2,1,0:T(8,128)(2,1)S(1)}, bf16[4,5,24,768]{3,2,1,0:T(8,128)(2,1)S(1)}, u32[]{:S(2)}, u32[]{:S(2)}) collective-permute-start(bf16[4,5,24,768]{3,2,1,0:T(8,128)(2,1)S(1)} %pad_maximum_fusion.1.refs_0_), channel_id=1, source_target_pairs={{0,1},{1,0},{2,6},{3,7},{4,5},{5,4},{6,2},{7,3},{8,9},{9,8},{10,14... | collective-permute-start | bytes 2211848 | tf_op jit(solution)/shard_map/ppermute | solution.py:73
  92.2 33.5 %collective-permute-start.21 = (bf16[4,5,24,768]{3,2,1,0:T(8,128)(2,1)S(1)}, bf16[4,5,24,768]{3,2,1,0:T(8,128)(2,1)S(1)}, u32[]{:S(2)}, u32[]{:S(2)}) collective-permute-start(bf16[4,5,24,768]{3,2,1,0:T(8,128)(2,1)S(1)} %pad_maximum_fusion.1.refs_0_), channel_id=1, source_target_pairs={{0,5},{1,4},{2,7},{3,6},{4,1},{5,0},{6,3},{7,2},{8,13},{9,12},{10,... | collective-permute-start | bytes 2211848 | tf_op jit(solution)/shard_map/ppermute | solution.py:73
  134.1 24.0 %collective-permute-start.30 = (bf16[1,64,768]{2,1,0:T(8,128)(2,1)S(1)}, bf16[1,64,768]{2,1,0:T(8,128)(2,1)S(1)}, u32[]{:S(2)}, u32[]{:S(2)}) collective-permute-start(bf16[1,64,768]{2,1,0:T(8,128)(2,1)S(1)} %get-tuple-element.282), channel_id=1, source_target_pairs={{0,8},{1,9},{2,10},{3,11},{4,12},{5,13},{6,14},{7,15},{8,16},{9,17... | collective-permute-start | bytes 294920 | tf_op jit(solution)/shard_map/ppermute | solution.py:73
  138.4 19.6 %collective-permute-start.31 = (bf16[1,64,768]{2,1,0:T(8,128)(2,1)S(1)}, bf16[1,64,768]{2,1,0:T(8,128)(2,1)S(1)}, u32[]{:S(2)}, u32[]{:S(2)}) collective-permute-start(bf16[1,64,768]{2,1,0:T(8,128)(2,1)S(1)} %get-tuple-element.282), channel_id=1, source_target_pairs={{0,16},{1,17},{2,18},{3,19},{4,20},{5,21},{6,22},{7,23},{8,24},{9,... | collective-permute-start | bytes 294920 | tf_op jit(solution)/shard_map/ppermute | solution.py:73
  138.9 19.1 %collective-permute-start.32 = (bf16[1,64,768]{2,1,0:T(8,128)(2,1)S(1)}, bf16[1,64,768]{2,1,0:T(8,128)(2,1)S(1)}, u32[]{:S(2)}, u32[]{:S(2)}) collective-permute-start(bf16[1,64,768]{2,1,0:T(8,128)(2,1)S(1)} %get-tuple-element.282), channel_id=1, source_target_pairs={{0,24},{1,25},{2,26},{3,27},{4,28},{5,29},{6,30},{7,31},{8,0},{9,1... | collective-permute-start | bytes 294920 | tf_op jit(solution)/shard_map/ppermute | solution.py:73
  216.1 35.2 %collective-permute-start.40 = (bf16[4,4,1,96,768]{4,3,2,1,0:T(8,128)(2,1)}, bf16[4,4,1,96,768]{4,3,2,1,0:T(8,128)(2,1)}, u32[]{:S(2)}, u32[]{:S(2)}) collective-permute-start(bf16[4,4,1,96,768]{4,3,2,1,0:T(8,128)(2,1)} %get-tuple-element.317), channel_id=1, source_target_pairs={{0,2},{1,3},{2,0},{3,1},{4,6},{5,7},{6,4},{7,5},{8,10},{9,11},{10,... | collective-permute-start | bytes 7077896 | tf_op jit(solution)/shard_map/ppermute | solution.py:73
  254.0 18.5 %collective-permute-start.41 = (bf16[2,4,1,96,768]{4,3,2,1,0:T(8,128)(2,1)S(1)}, bf16[2,4,1,96,768]{4,3,2,1,0:T(8,128)(2,1)S(1)}, u32[]{:S(2)}, u32[]{:S(2)}) collective-permute-start(bf16[2,4,1,96,768]{4,3,2,1,0:T(8,128)(2,1)S(1)} %add_convert_fusion.4), channel_id=1, source_target_pairs={{0,1},{1,0},{2,6},{3,7},{4,5},{5,4},{6,2},{7,3},{8,9},{9,8},{10,14... | collective-permute-start | bytes 3538952 | tf_op jit(solution)/shard_map/ppermute | solution.py:73
  287.8 16.3 %collective-permute-start.44 = (bf16[2,4,4,24,768]{4,3,2,1,0:T(8,128)(2,1)S(1)}, bf16[2,4,4,24,768]{4,3,2,1,0:T(8,128)(2,1)S(1)}, u32[]{:S(2)}, u32[]{:S(2)}) collective-permute-start(bf16[2,4,4,24,768]{4,3,2,1,0:T(8,128)(2,1)S(1)} %get-tuple-element.404), channel_id=1, source_target_pairs={{0,1},{1,0},{2,6},{3,7},{4,5},{5,4},{6,2},{7,3},{8,9},{9,8},{10,14... | collective-permute-start | bytes 3538952 | tf_op jit(solution)/shard_map/ppermute | solution.py:73
  310.4 22.2 %collective-permute-start.47 = (bf16[2,4,4,24,768]{4,3,2,1,0:T(8,128)(2,1)S(1)}, bf16[2,4,4,24,768]{4,3,2,1,0:T(8,128)(2,1)}, u32[]{:S(2)}, u32[]{:S(2)}) collective-permute-start(bf16[2,4,4,24,768]{4,3,2,1,0:T(8,128)(2,1)S(1)} %get-tuple-element.402), channel_id=1, source_target_pairs={{0,1},{1,0},{2,6},{3,7},{4,5},{5,4},{6,2},{7,3},{8,9},{9,8},{10,14... | collective-permute-start | bytes 3538952 | tf_op jit(solution)/shard_map/ppermute | solution.py:73
  311.1 16.4 %collective-permute-start.45 = (bf16[4,4,24,768]{3,2,1,0:T(8,128)(2,1)S(1)}, bf16[4,4,24,768]{3,2,1,0:T(8,128)(2,1)}, u32[]{:S(2)}, u32[]{:S(2)}) collective-permute-start(bf16[4,4,24,768]{3,2,1,0:T(8,128)(2,1)S(1)} %get-tuple-element.412), channel_id=1, source_target_pairs={{0,4},{1,5},{2,3},{3,2},{4,0},{5,1},{6,7},{7,6},{8,12},{9,13},{10,... | collective-permute-start | bytes 1769480 | tf_op jit(solution)/shard_map/ppermute | solution.py:73
  336.9 34.3 %collective-permute-start.49 = (bf16[4,4,24,768]{3,2,1,0:T(8,128)(2,1)S(1)}, bf16[4,4,24,768]{3,2,1,0:T(8,128)(2,1)S(1)}, u32[]{:S(2)}, u32[]{:S(2)}) collective-permute-start(bf16[4,4,24,768]{3,2,1,0:T(8,128)(2,1)S(1)} %get-tuple-element.409), channel_id=1, source_target_pairs={{0,4},{1,5},{2,3},{3,2},{4,0},{5,1},{6,7},{7,6},{8,12},{9,13},{10,... | collective-permute-start | bytes 1769480 | tf_op jit(solution)/shard_map/ppermute | solution.py:73
  343.2 18.7 %collective-permute-start.57 = (bf16[1,96,768]{2,1,0:T(8,128)(2,1)S(1)}, bf16[1,96,768]{2,1,0:T(8,128)(2,1)S(1)}, u32[]{:S(2)}, u32[]{:S(2)}) collective-permute-start(bf16[1,96,768]{2,1,0:T(8,128)(2,1)S(1)} %get-tuple-element.418), channel_id=1, source_target_pairs={{0,16},{1,17},{2,18},{3,19},{4,20},{5,21},{6,22},{7,23},{8,24},{9,... | collective-permute-start | bytes 442376 | tf_op jit(solution)/shard_map/ppermute | solution.py:73
  349.8 21.4 %collective-permute-start.58 = (bf16[1,96,768]{2,1,0:T(8,128)(2,1)S(1)}, bf16[1,96,768]{2,1,0:T(8,128)(2,1)S(1)}, u32[]{:S(2)}, u32[]{:S(2)}) collective-permute-start(bf16[1,96,768]{2,1,0:T(8,128)(2,1)S(1)} %get-tuple-element.417), channel_id=1, source_target_pairs={{0,24},{1,25},{2,26},{3,27},{4,28},{5,29},{6,30},{7,31},{8,0},{9,1... | collective-permute-start | bytes 442376 | tf_op jit(solution)/shard_map/ppermute | solution.py:73
  355.6 15.6 %collective-permute-start.50 = (bf16[4,2,24,768]{3,2,1,0:T(8,128)(2,1)S(1)}, bf16[4,2,24,768]{3,2,1,0:T(8,128)(2,1)S(1)}, u32[]{:S(2)}, u32[]{:S(2)}) collective-permute-start(bf16[4,2,24,768]{3,2,1,0:T(8,128)(2,1)S(1)} %get-tuple-element.407), channel_id=1, source_target_pairs={{0,4},{1,5},{2,3},{3,2},{4,0},{5,1},{6,7},{7,6},{8,12},{9,13},{10,... | collective-permute-start | bytes 884744 | tf_op jit(solution)/shard_map/ppermute | solution.py:73
  375.8 21.0 %collective-permute-start.59 = (bf16[4,24,768]{2,1,0:T(8,128)(2,1)S(1)}, bf16[4,24,768]{2,1,0:T(8,128)(2,1)S(1)}, u32[]{:S(2)}, u32[]{:S(2)}) collective-permute-start(bf16[4,24,768]{2,1,0:T(8,128)(2,1)S(1)} %get-tuple-element.415), channel_id=1, source_target_pairs={{0,8},{1,9},{2,10},{3,11},{4,12},{5,13},{6,14},{7,15},{8,16},{9,17... | collective-permute-start | bytes 442376 | tf_op jit(solution)/shard_map/ppermute | solution.py:73
  377.1 19.7 %collective-permute-start.60 = (bf16[4,24,768]{2,1,0:T(8,128)(2,1)S(1)}, bf16[4,24,768]{2,1,0:T(8,128)(2,1)S(1)}, u32[]{:S(2)}, u32[]{:S(2)}) collective-permute-start(bf16[4,24,768]{2,1,0:T(8,128)(2,1)S(1)} %get-tuple-element.414), channel_id=1, source_target_pairs={{0,16},{1,17},{2,18},{3,19},{4,20},{5,21},{6,22},{7,23},{8,24},{9,... | collective-permute-start | bytes 442376 | tf_op jit(solution)/shard_map/ppermute | solution.py:73
  377.9 18.9 %collective-permute-start.61 = (bf16[4,24,768]{2,1,0:T(8,128)(2,1)S(1)}, bf16[4,24,768]{2,1,0:T(8,128)(2,1)S(1)}, u32[]{:S(2)}, u32[]{:S(2)}) collective-permute-start(bf16[4,24,768]{2,1,0:T(8,128)(2,1)S(1)} %get-tuple-element.413), channel_id=1, source_target_pairs={{0,24},{1,25},{2,26},{3,27},{4,28},{5,29},{6,30},{7,31},{8,0},{9,1... | collective-permute-start | bytes 442376 | tf_op jit(solution)/shard_map/ppermute | solution.py:73
  380.8 15.5 %collective-permute-start.63 = (bf16[2,24,768]{2,1,0:T(8,128)(2,1)S(1)}, bf16[2,24,768]{2,1,0:T(8,128)(2,1)S(1)}, u32[]{:S(2)}, u32[]{:S(2)}) collective-permute-start(bf16[2,24,768]{2,1,0:T(8,128)(2,1)S(1)} %get-tuple-element.426), channel_id=1, source_target_pairs={{0,16},{1,17},{2,18},{3,19},{4,20},{5,21},{6,22},{7,23},{8,24},{9,... | collective-permute-start | bytes 221192 | tf_op jit(solution)/shard_map/ppermute | solution.py:73
  (116 other events, 1303.6 us)
